TPU v7x, 256 devices: a whole 4x4x8 slice. The times are simulated.
256 devices in a mesh: ctx: 32 (over y, z), tp: 8 (over x, core).
Axes of the slice: x: 4, y: 4, z: 8, core: 2. Of those that a mesh axis runs over, the one named last changes fastest.
Arguments:
- queries: bfloat16 [16384, 8192], P('ctx', 'tp'), may hold values from -6 to 6
- keys: bfloat16 [16384, 8192], P('ctx', 'tp'), may hold values from -6 to 6
- values: bfloat16 [16384, 8192], P('ctx', 'tp'), may hold values from -75 to 75
- gate: bfloat16 [16384, 8192], P('ctx', 'tp'), may hold values from -6 to 6
- gain: float32 [8192], P('tp'), may hold values from 0.1 to 1.9
- out_grad: bfloat16 [16384, 8192], P('ctx', 'tp'), may hold values from -6 to 6
Outputs:
- output: bfloat16 [16384, 8192], P('ctx', 'tp')
- query_grad: bfloat16 [16384, 8192], P('ctx', 'tp')
- key_grad: bfloat16 [16384, 8192], P('ctx', 'tp')
- value_grad: bfloat16 [16384, 8192], P('ctx', 'tp')
- gate_grad: bfloat16 [16384, 8192], P('ctx', 'tp')
All inputs are finite; a program needn't handle non-finite values.
Results may differ from a plain program's by a relative error of at most 0.005.
Values sent between devices are 32-bit elements; how exact they have to be, the bound alone decides.
No kernel may reach another device: no remote copies, remote signals or barrier semaphores. Data moves between devices by JAX's collectives and lax.ppermute only.
A program may use at most 128 MiB of HBM per device.

v0:
```python
import jax
import jax.numpy as jnp
from jax import lax
from jax.sharding import PartitionSpec as P

HD = 128
BLOCK = 512
D = 8192


EPS = 1e-06


def carried_in(value, axis, join, neutral, backward):
    count, mine = (lax.axis_size(axis), lax.axis_index(axis))
    pieces = lax.all_gather(value, axis)
    if backward:
        pieces = pieces[::-1]
        mine = count - 1 - mine
    running = jnp.full_like(value, 0) + jnp.asarray(neutral, value.dtype)

    def turn(position, running):
        longer = join(running, pieces[position])
        return jnp.where(position < mine, longer, running)

    return lax.fori_loop(0, count - 1, turn, running)


def add_states(earlier, later):
    return earlier + later


def local(queries, keys, values, gate, gain, out_grad):
    tok_rows, width = queries.shape
    heads_here = width // HD
    nblocks = tok_rows // BLOCK
    high = lax.Precision.HIGHEST

    def split(x):
        return x.reshape(nblocks, BLOCK, heads_here, HD)

    q_blocks, k_blocks, v_blocks = (split(queries), split(keys), split(values))
    row_ids = lax.broadcasted_iota(jnp.int32, (BLOCK, BLOCK), 0)
    col_ids = lax.broadcasted_iota(jnp.int32, (BLOCK, BLOCK), 1)
    causal = col_ids <= row_ids
    scores = jnp.einsum("nbhe,nche->nhbc", q_blocks, k_blocks, preferred_element_type=jnp.float32)
    attn = jnp.where(causal, scores, 0.0).astype(jnp.bfloat16)
    block_kv = jnp.einsum("nche,nchf->nhef", k_blocks, v_blocks, preferred_element_type=jnp.float32)
    device_kv = jnp.sum(block_kv, 0)
    local_before = jnp.cumsum(block_kv, 0) - block_kv
    empty = jnp.zeros_like(device_kv)
    carried = carried_in(device_kv, "ctx", add_states, empty, False)
    states = carried[None] + local_before
    inter = jnp.einsum("nbhe,nhef->nbhf", q_blocks.astype(jnp.float32), states, precision=high)
    intra = jnp.einsum("nhbc,nchf->nbhf", attn, v_blocks, preferred_element_type=jnp.float32)
    mixed = (intra + inter).reshape(tok_rows, width)
    sig = jax.nn.sigmoid(gate.astype(jnp.float32))
    dy_full = out_grad.astype(jnp.float32)
    dn = dy_full * gain * sig
    own_square = jnp.sum(mixed * mixed, axis=1)
    square_total = lax.psum(own_square, "tp")
    inv_rms = lax.rsqrt(square_total / D + EPS)[:, None]
    normed = mixed * inv_rms
    output = (normed * gain * sig).astype(jnp.bfloat16)
    cross_total = lax.psum(jnp.sum(dn * mixed, axis=1), "tp")
    project = inv_rms * (cross_total / D)[:, None]
    mixed_grad = (inv_rms * (dn - normed * project)).astype(jnp.bfloat16)
    gate_grad = (dy_full * gain * normed * sig * (1.0 - sig)).astype(jnp.bfloat16)
    d_blocks = split(mixed_grad)
    prob = jnp.where(
        causal,
        jnp.einsum("nbhf,nchf->nhbc", d_blocks, v_blocks, preferred_element_type=jnp.float32),
        0.0,
    ).astype(jnp.bfloat16)
    q_grad = jnp.einsum("nhbc,nche->nbhe", prob, k_blocks, preferred_element_type=jnp.float32)
    q_grad = q_grad + jnp.einsum(
        "nbhf,nhef->nbhe", d_blocks.astype(jnp.float32), states, precision=high
    )
    block_g = jnp.einsum("nbhe,nbhf->nhef", q_blocks, d_blocks, preferred_element_type=jnp.float32)
    local_after = jnp.flip(jnp.cumsum(jnp.flip(block_g, 0), 0), 0) - block_g
    device_g = jnp.sum(block_g, 0)
    later = carried_in(device_g, "ctx", add_states, empty, True)
    after = later[None] + local_after
    k_grad = jnp.einsum("nhbc,nbhe->nche", prob, q_blocks, preferred_element_type=jnp.float32)
    k_grad = k_grad + jnp.einsum(
        "nchf,nhef->nche", v_blocks.astype(jnp.float32), after, precision=high
    )
    v_grad = jnp.einsum("nhbc,nbhf->nchf", attn, d_blocks, preferred_element_type=jnp.float32)
    v_grad = v_grad + jnp.einsum(
        "nche,nhef->nchf", k_blocks.astype(jnp.float32), after, precision=high
    )
    return (
        output,
        q_grad.reshape(tok_rows, width).astype(jnp.bfloat16),
        k_grad.reshape(tok_rows, width).astype(jnp.bfloat16),
        v_grad.reshape(tok_rows, width).astype(jnp.bfloat16),
        gate_grad,
    )


def solution(mesh):
    return jax.shard_map(
        local,
        mesh=mesh,
        in_specs=(
            P("ctx", "tp"),
            P("ctx", "tp"),
            P("ctx", "tp"),
            P("ctx", "tp"),
            P("tp"),
            P("ctx", "tp"),
        ),
        out_specs=(P("ctx", "tp"), P("ctx", "tp"), P("ctx", "tp"), P("ctx", "tp"), P("ctx", "tp")),
        check_vma=False,
    )
```

profile of v0, /device:TPU:32, one launch (start us, length us, event | category | flops | bytes accessed | tf_op | source)
XLA Modules:
  0.0 431.5 jit_solution(13185674936705253317)
XLA Ops:
  7.2 2.6 copy.67
  9.8 1.6 copy.39
  11.4 2.9 fusion.9
  14.5 2.6 select_convert_fusion.1
  17.1 2.1 copy-done.1
  19.2 2.8 fusion.4
  22.1 133.8 %all-gather.5.cloned.1.call-done = f32[256,128,128]{2,1,0:T(8,128)} async-done(((f32[8,128,128]{2,1,0:T(8,128)}), f32[256,128,128]{2,1,0:T(8,128)}) %all-gather.5.cloned.1.call-update) | async-done | bytes 16777232 | tf_op jit(solution)/shard_map/all_gather | solution.py:16
  155.9 38.8 %while.28 = (s32[]{:T(128)}, f32[8,128,128]{2,1,0:T(8,128)S(1)}, s32[]{:T(128)}, f32[32,8,128,128]{3,2,1,0:T(8,128)}, s32[]{:T(128)}, /*index=5*/s32[]{:T(128)}) while((s32[]{:T(128)}, f32[8,128,128]{2,1,0:T(8,128)S(1)}, s32[]{:T(128)}, f32[32,8,128,128]{3,2,1,0:T(8,128)}, s32[]{:T(128)}, /*index=5*/s32[]{:T(128)}) %tuple.79), condition=%wide.region_1.2_spmd.clone, body=%wide.region_0.1_spmd.clone.sunk | while | flops 393220 | bytes 1572965 | solution.py:26
  155.9 1.3 add_select_fusion.4
  169.7 1.2 add_select_fusion.4
  179.7 1.2 add_select_fusion.4
  193.5 1.2 add_select_fusion.4
  194.7 4.1 fusion.2
  198.8 3.0 copy.43
  201.8 2.6 multiply_reduce_fusion
  204.4 14.4 %all-reduce = (f32[512]{0:T(512)S(1)}, f32[512]{0:T(512)S(1)}) all-reduce(f32[512]{0:T(512)S(1)} %get-tuple-element.228, f32[512]{0:T(512)S(1)} %multiply_reduce_fusion), channel_id=1, replica_groups=mesh['ctx'=32,'tp'=8] {'tp'}, use_global_device_ids=true, to_apply=%region_3.4 | all-reduce | flops 1024 | bytes 8192 | tf_op jit(solution)/shard_map/psum | solution.py:61
  218.7 4.9 %multiply_convert_fusion = (bf16[512,1024]{1,0:T(8,128)(2,1)}, bf16[512,1024]{1,0:T(8,128)(2,1)}, bf16[512,1024]{1,0:T(8,128)(2,1)}) fusion(bf16[512,1024]{1,0:T(8,128)(2,1)S(1)} %copy-done.14, f32[512,1024]{1,0:T(8,128)} %copy.43, f32[1024]{0:T(1024)S(1)} %copy-done.15, f32[512]{0:T(512)S(1)} %get-tuple-element.227, bf16[512,1024]{1,0:T(8,128)(2,1)} %param.13, ...), kind=kLoop, calls=%fused_computation.11 | loop fusion | flops 10485760 | bytes 7348224 | tf_op jit(solution)/shard_map/convert_element_type | solution.py:68
  223.6 1.5 copy.63
  226.6 2.7 select_convert_fusion
  229.4 1.5 fusion.27
  231.3 2.1 fusion.1
  233.4 2.3 copy.58
  235.7 4.5 %fusion.28 = f32[8,128,512]{2,1,0:T(8,128)} fusion(bf16[512,8,128]{0,2,1:T(8,128)(2,1)S(1)} %bitcast.119, bf16[8,512,512]{2,1,0:T(8,128)(2,1)} %copy-done.1), kind=kOutput, calls=%fused_computation.49 | convolution fusion | flops 536870912 | bytes 7340032 | tf_op jit(solution)/shard_map/nhbc,nbhf->nchf/dot_general | solution.py:88
  240.2 121.8 %all-gather.7.cloned.1.call-done = f32[256,128,128]{2,1,0:T(8,128)} async-done(((f32[8,128,128]{2,1,0:T(8,128)}), f32[256,128,128]{2,1,0:T(8,128)}) %all-gather.7.cloned.1.call-update) | async-done | bytes 16777232 | tf_op jit(solution)/shard_map/all_gather | solution.py:16
  361.9 11.7 %rev.3 = f32[32,8,128,128]{3,2,1,0:T(8,128)} reverse(f32[32,8,128,128]{3,2,1,0:T(8,128)} %bitcast.120), dimensions={0} | reverse | bytes 33554432 | tf_op jit(solution)/shard_map/rev | solution.py:18
  373.7 38.9 %while.29 = (s32[]{:T(128)}, f32[8,128,128]{2,1,0:T(8,128)S(1)}, s32[]{:T(128)}, f32[32,8,128,128]{3,2,1,0:T(8,128)}, s32[]{:T(128)}, /*index=5*/s32[]{:T(128)}) while((s32[]{:T(128)}, f32[8,128,128]{2,1,0:T(8,128)S(1)}, s32[]{:T(128)}, f32[32,8,128,128]{3,2,1,0:T(8,128)}, s32[]{:T(128)}, /*index=5*/s32[]{:T(128)}) %tuple.72), condition=%wide.region_7.8_spmd.clone, body=%wide.region_6.7_spmd.clone.sunk | while | flops 393220 | bytes 1572965 | solution.py:26
  373.7 1.3 add_select_fusion.5
  383.8 1.2 add_select_fusion.5
  413.6 3.6 fusion.6
  418.4 1.3 copy.60
  419.7 3.7 fusion
  423.4 1.3 copy.59
  (99 shorter events, 73.0 us)
Async XLA Ops:
  7.2 7.3 %copy-start = (bf16[512,1024]{1,0:T(8,128)(2,1)S(1)}, bf16[512,1024]{1,0:T(8,128)(2,1)}, u32[]{:S(2)}) copy-start(bf16[512,1024]{1,0:T(8,128)(2,1)} %param.10) | copy-start | bytes 3145732
  7.2 148.7 %all-gather.5.cloned.1.call-start = ((), (), s32[]{:S(2)}) async-start(), calls=%async_computation | async-start | bytes 17301504 | tf_op jit(solution)/shard_map/all_gather | solution.py:16
  11.4 5.7 %copy-start.3 = (bf16[512,8,128]{0,2,1:T(8,128)(2,1)}, bf16[512,8,128]{0,2,1:T(8,128)(2,1)S(1)}, u32[]{:S(2)}) copy-start(bf16[512,8,128]{0,2,1:T(8,128)(2,1)S(1)} %copy.39) | copy-start | bytes 3145732
  14.3 347.6 %all-gather.7.cloned.1.call-start = ((), (), s32[]{:S(2)}) async-start(), calls=%async_computation.1 | async-start | bytes 17301504 | tf_op jit(solution)/shard_map/all_gather | solution.py:16
  14.5 4.7 %copy-start.5 = (bf16[512,1024]{1,0:T(8,128)(2,1)S(1)}, bf16[512,1024]{1,0:T(8,128)(2,1)}, u32[]{:S(2)}) copy-start(bf16[512,1024]{1,0:T(8,128)(2,1)} %param.12) | copy-start | bytes 3145732
  17.1 2.1 copy-start.1
  155.9 38.8 %copy-start.7 = (f32[8,128,128]{2,1,0:T(8,128)S(1)}, f32[8,128,128]{2,1,0:T(8,128)}, u32[]{:S(2)}) copy-start(f32[8,128,128]{2,1,0:T(8,128)} %fusion.9) | copy-start | bytes 1572868
  198.8 3.0 copy-start.14
  198.8 3.0 copy-start.15
  225.6 1.0 copy-start.10
  226.6 2.7 copy-start.4
  229.4 2.0 copy-start.2
  229.4 2.0 copy-start.8
  373.6 39.9 %copy-start.6 = (bf16[512,1024]{1,0:T(8,128)(2,1)S(1)}, bf16[512,1024]{1,0:T(8,128)(2,1)}, u32[]{:S(2)}) copy-start(bf16[512,1024]{1,0:T(8,128)(2,1)} %param.12) | copy-start | bytes 3145732
  373.6 39.9 %copy-start.11 = (f32[8,128,128]{1,2,0:T(8,128)S(1)}, f32[8,128,128]{1,2,0:T(8,128)}, u32[]{:S(2)}) copy-start(f32[8,128,128]{1,2,0:T(8,128)} %copy-done.10) | copy-start | bytes 1572868
  413.6 3.6 copy-start.9
  413.6 3.6 copy-start.12
  413.6 3.6 copy-start.13
Sparse Core Ops, SparseCore 0:
  14.4 141.4 all-gather.4
  226.7 135.1 all-gather.6
where the time goes:
time: 437 us; the launch traced here: 432 us
  waiting for transfers between devices  256 us (59%)
  other arithmetic  83.8 us (19%)
  matrix products  32 us (7%)
  local copies, waits for them, and re-layouts  29.9 us (7%)
  blocking collectives  14.4 us (3%)
  between operations  14.3 us (3%)
    all_gather x2, waiting for transfers between devices, carried_in(): pieces = lax.all_gather(value, axis)  256 us
    select_n x62, other arithmetic, turn(): return jnp.where(position < mine, longer, running)  76.2 us
    psum x1, blocking collectives, local(): square_total = lax.psum(own_square, 'tp')  14.4 us
    rev x1, local copies, waits for them, and re-layouts, carried_in(): pieces = pieces[::-1]  11.7 us
    unnamed x36, local copies, waits for them, and re-layouts  10.1 us
  transfers between devices with their start and end apart: 2, of which 2 were waited for; matrix products, arithmetic and copies ran while one was open for 4% of the time, Pallas kernels for 0%

commit v1 on v0

v1 whole, which is shorter than its diff:
```python
import jax
import jax.numpy as jnp
from jax import lax
from jax.experimental import pallas as pl
from jax.experimental.pallas import tpu as pltpu
from jax.sharding import PartitionSpec as P

HD = 128
D = 8192
EPS = 1e-06
HALF = 256
PAIR = 2 * HD
F32 = jnp.float32
BF16 = jnp.bfloat16


def dot(a, b, dims):
    return lax.dot_general(a, b, (dims, ((), ())), preferred_element_type=F32)


def nn(a, b):
    return dot(a, b, ((1,), (0,)))


def nt(a, b):
    return dot(a, b, ((1,), (1,)))


def tn(a, b):
    return dot(a, b, ((0,), (0,)))


def halves(x):
    high = x.astype(BF16)
    return high, (x - high.astype(F32)).astype(BF16)


def causal_tile(x):
    rows = lax.broadcasted_iota(jnp.int32, x.shape, 0)
    cols = lax.broadcasted_iota(jnp.int32, x.shape, 1)
    return jnp.where(cols <= rows, x, 0.0)


def state_kernel(k_ref, v_ref, out_ref):
    for h in range(2):
        cols = slice(h * HD, (h + 1) * HD)
        out_ref[cols, :] = tn(k_ref[:, cols], v_ref[:, cols])


def scan_kernel(reverse, x_ref, out_ref):
    count = x_ref.shape[0]
    running = jnp.zeros(x_ref.shape[1:], F32)
    for step in range(count):
        i = count - 1 - step if reverse else step
        out_ref[i] = running
        running = running + x_ref[i]


def forward_kernel(q_ref, k_ref, v_ref, s_ref, gate_ref, gain_ref, dy_ref,
                   mixed_ref, attn_ref, sums_ref, square, cross):
    step = pl.program_id(0)

    @pl.when(step == 0)
    def _():
        square[...] = jnp.zeros_like(square)
        cross[...] = jnp.zeros_like(cross)

    for h in range(2):
        cols = slice(h * HD, (h + 1) * HD)
        q, k, v = q_ref[:, cols], k_ref[:, cols], v_ref[:, cols]
        q0, q1 = q[:HALF], q[HALF:]
        a00 = causal_tile(nt(q0, k[:HALF])).astype(BF16)
        a10 = nt(q1, k[:HALF]).astype(BF16)
        a11 = causal_tile(nt(q1, k[HALF:])).astype(BF16)
        attn_ref[h, 0] = a00
        attn_ref[h, 1] = a10
        attn_ref[h, 2] = a11
        high, low = halves(s_ref[cols, :])
        stacked = jnp.concatenate([high, low], 0)
        inter = nn(jnp.concatenate([q, q], 1), stacked)
        intra0 = nn(a00, v[:HALF])
        intra1 = nn(a10, v[:HALF]) + nn(a11, v[HALF:])
        mixed = jnp.concatenate([intra0, intra1], 0) + inter
        mixed_ref[:, cols] = mixed
        sig = jax.nn.sigmoid(gate_ref[:, cols].astype(F32))
        dn = dy_ref[:, cols].astype(F32) * gain_ref[:, cols] * sig
        square[...] += mixed * mixed
        cross[...] += dn * mixed

    @pl.when(step == pl.num_programs(0) - 1)
    def _():
        sums_ref[0:1, :] = jnp.sum(square[...].T, axis=0, keepdims=True)
        sums_ref[1:2, :] = jnp.sum(cross[...].T, axis=0, keepdims=True)


def norm_kernel(sums_ref, mixed_ref, gate_ref, gain_ref, dy_ref, q_ref,
                out_ref, ggrad_ref, d_ref, g_ref, inv_ref, proj_ref):
    @pl.when(pl.program_id(0) == 0)
    def _():
        total = sums_ref[...]
        inv = lax.rsqrt(total[0:1] / D + EPS)
        proj = inv * (total[1:2] / D)
        inv_ref[...] = jnp.broadcast_to(inv, (HD, inv.shape[1])).T
        proj_ref[...] = jnp.broadcast_to(proj, (HD, proj.shape[1])).T

    for h in range(2):
        cols = slice(h * HD, (h + 1) * HD)
        inv, proj = inv_ref[...], proj_ref[...]
        sig = jax.nn.sigmoid(gate_ref[:, cols].astype(F32))
        dy_gain = dy_ref[:, cols].astype(F32) * gain_ref[:, cols]
        normed = mixed_ref[:, cols] * inv
        out_ref[:, cols] = (normed * gain_ref[:, cols] * sig).astype(BF16)
        dn = dy_gain * sig
        grad = (inv * (dn - normed * proj)).astype(BF16)
        ggrad_ref[:, cols] = (dy_gain * normed * sig * (1.0 - sig)).astype(BF16)
        d_ref[:, cols] = grad
        g_ref[cols, :] = tn(q_ref[:, cols], grad)


def backward_kernel(q_ref, k_ref, v_ref, d_ref, attn_ref, s_ref, after_ref,
                    qg_ref, kg_ref, vg_ref):
    for h in range(2):
        cols = slice(h * HD, (h + 1) * HD)
        q, k, v, d = q_ref[:, cols], k_ref[:, cols], v_ref[:, cols], d_ref[:, cols]
        d0, d1, q0, q1 = d[:HALF], d[HALF:], q[:HALF], q[HALF:]
        p00 = causal_tile(nt(d0, v[:HALF])).astype(BF16)
        p10 = nt(d1, v[:HALF]).astype(BF16)
        p11 = causal_tile(nt(d1, v[HALF:])).astype(BF16)
        a00, a10, a11 = attn_ref[h, 0], attn_ref[h, 1], attn_ref[h, 2]
        s_pair = jnp.concatenate(halves(s_ref[cols, :]), 1)
        after_high, after_low = halves(after_ref[cols, :])
        q_inter = nt(jnp.concatenate([d, d], 1), s_pair)
        k_inter = nt(jnp.concatenate([v, v], 1), jnp.concatenate([after_high, after_low], 1))
        v_inter = nn(jnp.concatenate([k, k], 1), jnp.concatenate([after_high, after_low], 0))
        q_intra0 = nn(p00, k[:HALF])
        q_intra1 = nn(p10, k[:HALF]) + nn(p11, k[HALF:])
        k_intra0 = tn(p00, q0) + tn(p10, q1)
        k_intra1 = tn(p11, q1)
        v_intra0 = tn(a00, d0) + tn(a10, d1)
        v_intra1 = tn(a11, d1)
        qg_ref[:HALF, cols] = (q_intra0 + q_inter[:HALF]).astype(BF16)
        qg_ref[HALF:, cols] = (q_intra1 + q_inter[HALF:]).astype(BF16)
        kg_ref[:HALF, cols] = (k_intra0 + k_inter[:HALF]).astype(BF16)
        kg_ref[HALF:, cols] = (k_intra1 + k_inter[HALF:]).astype(BF16)
        vg_ref[:HALF, cols] = (v_intra0 + v_inter[:HALF]).astype(BF16)
        vg_ref[HALF:, cols] = (v_intra1 + v_inter[HALF:]).astype(BF16)


def params():
    return pltpu.CompilerParams(
        dimension_semantics=("arbitrary",), vmem_limit_bytes=48 * 2**20
    )


def carried_in(value, reverse):
    count = lax.axis_size("ctx")
    rows = value.shape[0] // count
    mine = lax.all_to_all(value.reshape(count, rows, HD), "ctx", 0, 0)
    summed = pl.pallas_call(
        lambda x, o: scan_kernel(reverse, x, o),
        out_shape=jax.ShapeDtypeStruct(mine.shape, F32),
        in_specs=[pl.BlockSpec(memory_space=pltpu.VMEM)],
        out_specs=pl.BlockSpec(memory_space=pltpu.VMEM),
        name="suffix" if reverse else "prefix",
    )(mine)
    return lax.all_to_all(summed, "ctx", 0, 0).reshape(value.shape)


def tp_sum(x):
    n = lax.axis_size("tp")
    for flip in (1, 2, 4):
        x = x + lax.ppermute(x, "tp", [(i, i ^ flip) for i in range(n)])
    return x


def local(queries, keys, values, gate, gain, out_grad):
    rows, width = queries.shape
    steps = width // PAIR
    gain_row = gain.reshape(1, width)
    wide = pl.BlockSpec((rows, PAIR), lambda i: (0, i))
    gain_spec = pl.BlockSpec((1, PAIR), lambda i: (0, i))
    state = pl.BlockSpec((PAIR, HD), lambda i: (i, 0))
    tiles = pl.BlockSpec((2, 3, HALF, HALF), lambda i: (i, 0, 0, 0))
    sums_spec = pl.BlockSpec((2, rows), lambda i: (0, 0))
    half_shape = jax.ShapeDtypeStruct((rows, width), BF16)
    state_shape = jax.ShapeDtypeStruct((width, HD), F32)

    own = pl.pallas_call(
        state_kernel, grid=(steps,), in_specs=[wide, wide], out_specs=state,
        out_shape=state_shape, compiler_params=params(), name="state",
    )(keys, values)
    states = carried_in(own, False)

    mixed, attn, sums = pl.pallas_call(
        forward_kernel,
        grid=(steps,),
        in_specs=[wide, wide, wide, state, wide, gain_spec, wide],
        out_specs=[wide, tiles, sums_spec],
        out_shape=[
            jax.ShapeDtypeStruct((rows, width), F32),
            jax.ShapeDtypeStruct((width // HD, 3, HALF, HALF), BF16),
            jax.ShapeDtypeStruct((2, rows), F32),
        ],
        scratch_shapes=[pltpu.VMEM((rows, HD), F32), pltpu.VMEM((rows, HD), F32)],
        compiler_params=params(), name="forward",
    )(queries, keys, values, states, gate, gain_row, out_grad)
    total = tp_sum(sums)

    output, gate_grad, mixed_grad, own_after = pl.pallas_call(
        norm_kernel,
        grid=(steps,),
        in_specs=[sums_spec, wide, wide, gain_spec, wide, wide],
        out_specs=[wide, wide, wide, state],
        out_shape=[half_shape, half_shape, half_shape, state_shape],
        scratch_shapes=[pltpu.VMEM((rows, HD), F32), pltpu.VMEM((rows, HD), F32)],
        compiler_params=params(), name="norm",
    )(total, mixed, gate, gain_row, out_grad, queries)
    after = carried_in(own_after, True)

    q_grad, k_grad, v_grad = pl.pallas_call(
        backward_kernel,
        grid=(steps,),
        in_specs=[wide, wide, wide, wide, tiles, state, state],
        out_specs=[wide, wide, wide],
        out_shape=[half_shape, half_shape, half_shape],
        compiler_params=params(), name="backward",
    )(queries, keys, values, mixed_grad, attn, states, after)
    return output, q_grad, k_grad, v_grad, gate_grad


def solution(mesh):
    wide = P("ctx", "tp")
    return jax.shard_map(
        local,
        mesh=mesh,
        in_specs=(wide, wide, wide, wide, P("tp"), wide),
        out_specs=(wide, wide, wide, wide, wide),
        check_vma=False,
    )
```

time: 437 us -> 134 us (0.31); the launches traced: 432 us -> 133 us
  waiting for transfers between devices: 256 us -> 5.36 us
  other arithmetic: 83.8 us -> 0.01 us
  blocking collectives: 14.4 us -> 91.2 us
  matrix products: 32 us -> 0 us
  Pallas kernels: 0 us -> 23.3 us
  local copies, waits for them, and re-layouts: 29.9 us -> 8.42 us
  between operations: 14.3 us -> 0.7 us
  starting transfers between devices: 0.08 us -> 4.53 us
    all_gather x2 -> x0, waiting for transfers between devices: 256 us -> none  [carried_in(): pieces = lax.all_gather(value, axis)]
    all_to_all x0 -> x4, blocking collectives: none -> 91.2 us  [the longest x2 49.3 us: carried_in(): mine = lax.all_to_all(value.reshape(count, rows, HD), 'ctx', 0, 0)]
    select_n x62 -> x0, other arithmetic: 76.2 us -> none  [turn(): return jnp.where(position < mine, longer, running)]
    dot_general x12 -> x0, matrix products: 32 us -> none  [the longest x1 4.47 us: local(): jnp.einsum('nhbc,nbhf->nchf', attn, d_blocks, preferred_element_type=jnp....]
    pallas_call x0 -> x6, Pallas kernels: none -> 23.3 us  [the longest x1 8.03 us: local(): pl.pallas_call(backward_kernel, grid=(steps,), in_specs=[wide, wide, wide...]
    psum x1 -> x0, blocking collectives: 14.4 us -> none  [local(): square_total = lax.psum(own_square, 'tp')]
    rev x1 -> x0, local copies, waits for them, and re-layouts: 11.7 us -> none  [carried_in(): pieces = pieces[::-1]]
    ppermute x0 -> x3, waiting for transfers between devices: none -> 5.36 us  [tp_sum(): x = x + lax.ppermute(x, 'tp', [(i, i ^ flip) for i in range(n)])]
  transfers between devices with their start and end apart: 2 -> 3, of which waited for: 2 -> 3; matrix products, arithmetic and copies ran while one was open for 4% -> 0% of each run, Pallas kernels for 0% -> 0%
where the time goes in v1:
time: 134 us; the launch traced here: 133 us
  blocking collectives  91.2 us (68%)
  Pallas kernels  23.3 us (17%)
  local copies, waits for them, and re-layouts  8.42 us (6%)
  waiting for transfers between devices  5.36 us (4%)
  starting transfers between devices  4.53 us (3%)
    all_to_all x2, blocking collectives, carried_in(): mine = lax.all_to_all(value.reshape(count, rows, HD), 'ctx', 0, 0)  49.3 us
    all_to_all x2, blocking collectives, carried_in(): return lax.all_to_all(summed, 'ctx', 0, 0).reshape(value.shape)  41.9 us
    unnamed x26, local copies, waits for them, and re-layouts  8.42 us
    pallas_call x1, Pallas kernels, local(): pl.pallas_call(backward_kernel, grid=(steps,), in_specs=[wide, wide, wide...  8.03 us
    ppermute x3, waiting for transfers between devices, tp_sum(): x = x + lax.ppermute(x, 'tp', [(i, i ^ flip) for i in range(n)])  5.36 us
    pallas_call x1, Pallas kernels, local(): pl.pallas_call(forward_kernel, grid=(steps,), in_specs=[wide, wide, wide,...  5.29 us
    pallas_call x1, Pallas kernels, local(): pl.pallas_call(norm_kernel, grid=(steps,), in_specs=[sums_spec, wide, wid...  4.78 us
    ppermute x3, starting transfers between devices, tp_sum(): x = x + lax.ppermute(x, 'tp', [(i, i ^ flip) for i in range(n)])  4.53 us
  transfers between devices with their start and end apart: 3, of which 3 were waited for; matrix products, arithmetic and copies ran while one was open for 0% of the time, Pallas kernels for 0%

profile of v1, /device:TPU:32, one launch (start us, length us, event | category | flops | bytes accessed | tf_op | source)
XLA Modules:
  0.0 133.5 jit_solution(596625771259482770)
XLA Ops:
  0.6 0.0 copy-start
  0.6 0.0 copy-start.1
  0.7 1.3 copy-done.1
  2.0 1.2 copy-done.3
  3.2 1.4 %state.1 = f32[1024,128]{1,0:T(8,128)S(1)} custom-call(bf16[512,1024]{1,0:T(8,128)(2,1)S(1)} %copy-done.1, bf16[512,1024]{1,0:T(8,128)(2,1)S(1)} %copy-done.3), custom_call_target="tpu_custom_call" | custom-call | tf_op jit(solution)/shard_map/state/pallas_call | solution.py:188
  4.6 28.9 %all_to_all.20.x = f32[32,32,128]{2,1,0:T(8,128)} all-to-all(f32[32,32,128]{2,1,0:T(8,128)S(1)} %bitcast.8), channel_id=1, replica_groups=mesh['ctx'=32,'tp'=8] {'ctx'}, dimensions={0} | all-to-all | bytes 1048576 | tf_op jit(solution)/shard_map/all_to_all | solution.py:158
  33.5 1.9 %prefix.1 = f32[32,32,128]{2,1,0:T(8,128)} custom-call(f32[32,32,128]{2,1,0:T(8,128)} %all_to_all.20.x), custom_call_target="tpu_custom_call" | custom-call | tf_op jit(solution)/shard_map/prefix/pallas_call | solution.py:159
  35.4 21.9 %all_to_all.21 = f32[32,32,128]{2,1,0:T(8,128)S(1)} all-to-all(f32[32,32,128]{2,1,0:T(8,128)} %prefix.1), channel_id=1, replica_groups=mesh['ctx'=32,'tp'=8] {'ctx'}, dimensions={0} | all-to-all | bytes 1048576 | tf_op jit(solution)/shard_map/all_to_all | solution.py:166
  57.3 0.0 copy-done
  57.3 0.0 copy-done.2
  57.3 0.0 copy-done.4
  57.3 0.0 copy-done.12
  57.3 0.0 copy-start.7
  57.3 1.4 %copy-done.7 = bf16[512,1024]{1,0:T(8,128)(2,1)S(1)} copy-done((bf16[512,1024]{1,0:T(8,128)(2,1)S(1)}, bf16[512,1024]{1,0:T(8,128)(2,1)}, u32[]{:S(2)}) %copy-start.7) | copy-done | bytes 1048600
  58.7 1.2 copy-done.8
  60.0 5.3 %forward.1 = (f32[512,1024]{1,0:T(8,128)}, bf16[8,3,256,256]{3,2,1,0:T(8,128)(2,1)}, f32[2,512]{1,0:T(2,128)S(1)}) custom-call(bf16[512,1024]{1,0:T(8,128)(2,1)S(1)} %copy-done, bf16[512,1024]{1,0:T(8,128)(2,1)S(1)} %copy-done.2, bf16[512,1024]{1,0:T(8,128)(2,1)S(1)} %copy-done.4, f32[1024,128]{1,0:T(8,128)S(1)} %bitcast.5, bf16[512,1024]{1,0:T(8,128)(2,1)S(1)} %copy-done.7, ...), custom_call_target="tpu_custom_call" | custom-call | tf_op jit(solution)/shard_map/forward/pallas_call | solution.py:194
  65.3 0.0 collective-permute-start
  65.3 1.2 collective-permute-done
  66.4 1.5 %collective-permute-start.1 = (f32[2,512]{1,0:T(2,128)S(1)}, f32[2,512]{1,0:T(2,128)S(1)}, u32[]{:S(2)}, u32[]{:S(2)}) collective-permute-start(f32[2,512]{1,0:T(2,128)S(1)} %add.9), channel_id=1, source_target_pairs={{0,2},{1,3},{2,0},{3,1},{4,6},{5,7},{6,4},{7,5},{8,10},{9,11},{10,... | collective-permute-start | bytes 12296 | tf_op jit(solution)/shard_map/ppermute | solution.py:172
  67.9 2.1 %collective-permute-done.1 = f32[2,512]{1,0:T(2,128)S(1)} collective-permute-done((f32[2,512]{1,0:T(2,128)S(1)}, f32[2,512]{1,0:T(2,128)S(1)}, u32[]{:S(2)}, u32[]{:S(2)}) %collective-permute-start.1) | collective-permute-done | bytes 4128 | tf_op jit(solution)/shard_map/ppermute | solution.py:172
  70.0 3.0 %collective-permute-start.2 = (f32[2,512]{1,0:T(2,128)S(1)}, f32[2,512]{1,0:T(2,128)S(1)}, u32[]{:S(2)}, u32[]{:S(2)}) collective-permute-start(f32[2,512]{1,0:T(2,128)S(1)} %add.10), channel_id=1, source_target_pairs={{0,4},{1,5},{2,6},{3,7},{4,0},{5,1},{6,2},{7,3},{8,12},{9,13},{10,... | collective-permute-start | bytes 12296 | tf_op jit(solution)/shard_map/ppermute | solution.py:172
  73.1 2.1 %collective-permute-done.2 = f32[2,512]{1,0:T(2,128)S(1)} collective-permute-done((f32[2,512]{1,0:T(2,128)S(1)}, f32[2,512]{1,0:T(2,128)S(1)}, u32[]{:S(2)}, u32[]{:S(2)}) %collective-permute-start.2) | collective-permute-done | bytes 4128 | tf_op jit(solution)/shard_map/ppermute | solution.py:172
  75.2 0.0 copy-done.9
  75.2 4.8 %norm.1 = (bf16[512,1024]{1,0:T(8,128)(2,1)}, bf16[512,1024]{1,0:T(8,128)(2,1)}, bf16[512,1024]{1,0:T(8,128)(2,1)S(1)}, f32[1024,128]{1,0:T(8,128)S(1)}) custom-call(f32[2,512]{1,0:T(2,128)S(1)} %add.11.sums_ref, f32[512,1024]{1,0:T(8,128)} %get-tuple-element.16.mixed_ref, bf16[512,1024]{1,0:T(8,128)(2,1)S(1)} %copy-done.7, f32[1,1024]{1,0:T(1,128)S(1)} %bitcast.11, ...), custom_call_target="tpu_custom_call" | custom-call | tf_op jit(solution)/shard_map/norm/pallas_call | solution.py:209
  79.9 0.0 copy-done.5
  80.0 1.0 copy-done.10
  80.9 20.4 %all_to_all.22.x = f32[32,32,128]{2,1,0:T(8,128)} all-to-all(f32[32,32,128]{2,1,0:T(8,128)S(1)} %bitcast.9), channel_id=1, replica_groups=mesh['ctx'=32,'tp'=8] {'ctx'}, dimensions={0} | all-to-all | bytes 1048576 | tf_op jit(solution)/shard_map/all_to_all | solution.py:158
  101.3 1.9 %suffix.1 = f32[32,32,128]{2,1,0:T(8,128)} custom-call(f32[32,32,128]{2,1,0:T(8,128)} %all_to_all.22.x), custom_call_target="tpu_custom_call" | custom-call | tf_op jit(solution)/shard_map/suffix/pallas_call | solution.py:159
  103.2 20.0 %all_to_all.23 = f32[32,32,128]{2,1,0:T(8,128)S(1)} all-to-all(f32[32,32,128]{2,1,0:T(8,128)} %suffix.1), channel_id=1, replica_groups=mesh['ctx'=32,'tp'=8] {'ctx'}, dimensions={0} | all-to-all | bytes 1048576 | tf_op jit(solution)/shard_map/all_to_all | solution.py:166
  123.2 1.0 copy-done.6
  124.2 1.2 copy-done.11
  125.5 8.0 %backward.1 = (bf16[512,1024]{1,0:T(8,128)(2,1)}, bf16[512,1024]{1,0:T(8,128)(2,1)}, bf16[512,1024]{1,0:T(8,128)(2,1)}) custom-call(bf16[512,1024]{1,0:T(8,128)(2,1)S(1)} %copy-done, bf16[512,1024]{1,0:T(8,128)(2,1)S(1)} %copy-done.2, bf16[512,1024]{1,0:T(8,128)(2,1)S(1)} %copy-done.4, bf16[512,1024]{1,0:T(8,128)(2,1)S(1)} %copy-done.11, ...), custom_call_target="tpu_custom_call" | custom-call | tf_op jit(solution)/shard_map/backward/pallas_call | solution.py:220
  (13 shorter events, 0.0 us)
Async XLA Ops:
  0.6 56.7 %copy-start = (bf16[512,1024]{1,0:T(8,128)(2,1)S(1)}, bf16[512,1024]{1,0:T(8,128)(2,1)}, u32[]{:S(2)}) copy-start(bf16[512,1024]{1,0:T(8,128)(2,1)} %q_ref.5) | copy-start | bytes 3145732
  0.6 1.3 copy-start.1
  2.0 1.2 copy-start.3
  3.2 54.1 %copy-start.2 = (bf16[512,1024]{1,0:T(8,128)(2,1)S(1)}, bf16[512,1024]{1,0:T(8,128)(2,1)}, u32[]{:S(2)}) copy-start(bf16[512,1024]{1,0:T(8,128)(2,1)} %k_ref.5) | copy-start | bytes 3145732
  3.2 54.1 %copy-start.4 = (bf16[512,1024]{1,0:T(8,128)(2,1)S(1)}, bf16[512,1024]{1,0:T(8,128)(2,1)}, u32[]{:S(2)}) copy-start(bf16[512,1024]{1,0:T(8,128)(2,1)} %v_ref.5) | copy-start | bytes 3145732
  3.2 54.1 %copy-start.12 = (f32[1024]{0:T(1024)S(1)}, f32[1024]{0:T(1024)}, u32[]{:S(2)}) copy-start(f32[1024]{0:T(1024)} %param.10) | copy-start | bytes 12292
  35.4 39.8 %copy-start.9 = (bf16[512,1024]{1,0:T(8,128)(2,1)S(1)}, bf16[512,1024]{1,0:T(8,128)(2,1)}, u32[]{:S(2)}) copy-start(bf16[512,1024]{1,0:T(8,128)(2,1)} %dy_ref.3) | copy-start | bytes 3145732
  57.3 22.6 %copy-start.5 = (f32[32,32,128]{2,1,0:T(8,128)}, f32[32,32,128]{2,1,0:T(8,128)S(1)}, u32[]{:S(2)}) copy-start(f32[32,32,128]{2,1,0:T(8,128)S(1)} %all_to_all.21) | copy-start | bytes 1572868
  57.3 1.4 %copy-start.7 = (bf16[512,1024]{1,0:T(8,128)(2,1)S(1)}, bf16[512,1024]{1,0:T(8,128)(2,1)}, u32[]{:S(2)}) copy-start(bf16[512,1024]{1,0:T(8,128)(2,1)} %gate_ref.3) | copy-start | bytes 3145732
  58.7 1.2 copy-start.8
  65.3 1.2 collective-permute-start
  66.4 3.6 %collective-permute-start.1 = (f32[2,512]{1,0:T(2,128)S(1)}, f32[2,512]{1,0:T(2,128)S(1)}, u32[]{:S(2)}, u32[]{:S(2)}) collective-permute-start(f32[2,512]{1,0:T(2,128)S(1)} %add.9), channel_id=1, source_target_pairs={{0,2},{1,3},{2,0},{3,1},{4,6},{5,7},{6,4},{7,5},{8,10},{9,11},{10,... | collective-permute-start | bytes 12296 | tf_op jit(solution)/shard_map/ppermute | solution.py:172
  70.0 5.1 %collective-permute-start.2 = (f32[2,512]{1,0:T(2,128)S(1)}, f32[2,512]{1,0:T(2,128)S(1)}, u32[]{:S(2)}, u32[]{:S(2)}) collective-permute-start(f32[2,512]{1,0:T(2,128)S(1)} %add.10), channel_id=1, source_target_pairs={{0,4},{1,5},{2,6},{3,7},{4,0},{5,1},{6,2},{7,3},{8,12},{9,13},{10,... | collective-permute-start | bytes 12296 | tf_op jit(solution)/shard_map/ppermute | solution.py:172
  80.0 1.0 copy-start.10
  123.2 1.0 copy-start.6
  124.2 1.2 copy-start.11

commit v2 on v1

v2 whole, which is shorter than its diff:
```python
import jax
import jax.numpy as jnp
from jax import lax
from jax.experimental import pallas as pl
from jax.experimental.pallas import tpu as pltpu
from jax.sharding import PartitionSpec as P

HD = 128
D = 8192
EPS = 1e-06
HALF = 256
PAIR = 2 * HD
F32 = jnp.float32
BF16 = jnp.bfloat16


def dot(a, b, dims):
    return lax.dot_general(a, b, (dims, ((), ())), preferred_element_type=F32)


def nn(a, b):
    return dot(a, b, ((1,), (0,)))


def nt(a, b):
    return dot(a, b, ((1,), (1,)))


def tn(a, b):
    return dot(a, b, ((0,), (0,)))


def halves(x):
    high = x.astype(BF16)
    return high, (x - high.astype(F32)).astype(BF16)


def causal_tile(x):
    rows = lax.broadcasted_iota(jnp.int32, x.shape, 0)
    cols = lax.broadcasted_iota(jnp.int32, x.shape, 1)
    return jnp.where(cols <= rows, x, 0.0)


def fetch(source, target, sems, width):
    copies = []
    for i in range(source.shape[1] // width):
        cols = pl.ds(i * width, width)
        copy = pltpu.make_async_copy(source.at[:, cols], target.at[:, cols], sems.at[i])
        copy.start()
        copies.append(copy)
    return copies


def state_kernel(k_ref, v_ref, out_ref, k_buf, v_buf, k_sem, v_sem):
    k_copies = fetch(k_ref, k_buf, k_sem, PAIR)
    v_copies = fetch(v_ref, v_buf, v_sem, PAIR)
    for i in range(len(k_copies)):
        k_copies[i].wait()
        v_copies[i].wait()
        for h in (2 * i, 2 * i + 1):
            cols = slice(h * HD, (h + 1) * HD)
            out_ref[cols, :] = tn(k_buf[:, cols], v_buf[:, cols])


def scan_kernel(reverse, x_ref, out_ref):
    count = x_ref.shape[0]
    running = jnp.zeros(x_ref.shape[1:], F32)
    for step in range(count):
        i = count - 1 - step if reverse else step
        out_ref[i] = running
        running = running + x_ref[i]


def forward_kernel(q_ref, k_ref, v_ref, s_ref, gain_ref, gate_ref, dy_ref,
                   mixed_ref, sums_ref, square, cross):
    heads = q_ref.shape[1] // HD
    for h in range(heads):
        cols = slice(h * HD, (h + 1) * HD)
        q, k, v = q_ref[:, cols], k_ref[:, cols], v_ref[:, cols]
        q0, q1 = q[:HALF], q[HALF:]
        a00 = causal_tile(nt(q0, k[:HALF])).astype(BF16)
        a10 = nt(q1, k[:HALF]).astype(BF16)
        a11 = causal_tile(nt(q1, k[HALF:])).astype(BF16)
        inter = nn(jnp.concatenate([q, q], 1), jnp.concatenate(halves(s_ref[cols, :]), 0))
        mixed_ref[:HALF, cols] = nn(a00, v[:HALF]) + inter[:HALF]
        mixed_ref[HALF:, cols] = nn(a10, v[:HALF]) + nn(a11, v[HALF:]) + inter[HALF:]
    square[...] = jnp.zeros_like(square)
    cross[...] = jnp.zeros_like(cross)
    for h in range(heads):
        cols = slice(h * HD, (h + 1) * HD)
        mixed = mixed_ref[:, cols]
        sig = jax.nn.sigmoid(gate_ref[:, cols].astype(F32))
        dn = dy_ref[:, cols].astype(F32) * gain_ref[:, cols] * sig
        square[...] += mixed * mixed
        cross[...] += dn * mixed
    sums_ref[0:1, :] = jnp.sum(square[...].T, axis=0, keepdims=True)
    sums_ref[1:2, :] = jnp.sum(cross[...].T, axis=0, keepdims=True)


def norm_kernel(sums_ref, mixed_ref, gate_ref, gain_ref, dy_ref, q_ref,
                out_ref, ggrad_ref, d_ref, g_ref,
                out_buf, ggrad_buf, inv_ref, proj_ref, sems):
    total = sums_ref[...]
    inv = lax.rsqrt(total[0:1] / D + EPS)
    proj = inv * (total[1:2] / D)
    inv_ref[...] = jnp.broadcast_to(inv, (HD, inv.shape[1])).T
    proj_ref[...] = jnp.broadcast_to(proj, (HD, proj.shape[1])).T
    copies = []
    for h in range(q_ref.shape[1] // HD):
        cols = slice(h * HD, (h + 1) * HD)
        inv, proj = inv_ref[...], proj_ref[...]
        sig = jax.nn.sigmoid(gate_ref[:, cols].astype(F32))
        gain = gain_ref[:, cols]
        gain_sig = gain * sig
        dn = dy_ref[:, cols].astype(F32) * gain_sig
        normed = mixed_ref[:, cols] * inv
        out_buf[:, cols] = (normed * gain_sig).astype(BF16)
        grad = (inv * (dn - normed * proj)).astype(BF16)
        ggrad_buf[:, cols] = (dn * normed * (1.0 - sig)).astype(BF16)
        d_ref[:, cols] = grad
        g_ref[cols, :] = tn(q_ref[:, cols], grad)
        if h % 2 == 1:
            both = pl.ds((h - 1) * HD, PAIR)
            for j, (buf, ref) in enumerate(((out_buf, out_ref), (ggrad_buf, ggrad_ref))):
                copy = pltpu.make_async_copy(buf.at[:, both], ref.at[:, both], sems.at[j, h // 2])
                copy.start()
                copies.append(copy)
    for copy in copies:
        copy.wait()


def backward_kernel(q_ref, k_ref, v_ref, after_ref, s_ref, d_ref,
                    qg_ref, kg_ref, vg_ref, qg_buf, kg_buf, vg_buf, sems):
    copies = []
    for h in range(q_ref.shape[1] // HD):
        cols = slice(h * HD, (h + 1) * HD)
        q, k, v, d = q_ref[:, cols], k_ref[:, cols], v_ref[:, cols], d_ref[:, cols]
        d0, d1, q0, q1 = d[:HALF], d[HALF:], q[:HALF], q[HALF:]
        p00 = causal_tile(nt(d0, v[:HALF])).astype(BF16)
        p10 = nt(d1, v[:HALF]).astype(BF16)
        p11 = causal_tile(nt(d1, v[HALF:])).astype(BF16)
        a00 = causal_tile(nt(q0, k[:HALF])).astype(BF16)
        a10 = nt(q1, k[:HALF]).astype(BF16)
        a11 = causal_tile(nt(q1, k[HALF:])).astype(BF16)
        after_high, after_low = halves(after_ref[cols, :])
        after_wide = jnp.concatenate([after_high, after_low], 1)
        after_tall = jnp.concatenate([after_high, after_low], 0)
        q_inter = nt(jnp.concatenate([d, d], 1), jnp.concatenate(halves(s_ref[cols, :]), 1))
        k_inter = nt(jnp.concatenate([v, v], 1), after_wide)
        v_inter = nn(jnp.concatenate([k, k], 1), after_tall)
        qg_buf[:HALF, cols] = (nn(p00, k[:HALF]) + q_inter[:HALF]).astype(BF16)
        qg_buf[HALF:, cols] = (nn(p10, k[:HALF]) + nn(p11, k[HALF:]) + q_inter[HALF:]).astype(BF16)
        kg_buf[:HALF, cols] = (tn(p00, q0) + tn(p10, q1) + k_inter[:HALF]).astype(BF16)
        kg_buf[HALF:, cols] = (tn(p11, q1) + k_inter[HALF:]).astype(BF16)
        vg_buf[:HALF, cols] = (tn(a00, d0) + tn(a10, d1) + v_inter[:HALF]).astype(BF16)
        vg_buf[HALF:, cols] = (tn(a11, d1) + v_inter[HALF:]).astype(BF16)
        if h % 2 == 1:
            both = pl.ds((h - 1) * HD, PAIR)
            for j, (buf, ref) in enumerate(((qg_buf, qg_ref), (kg_buf, kg_ref), (vg_buf, vg_ref))):
                copy = pltpu.make_async_copy(buf.at[:, both], ref.at[:, both], sems.at[j, h // 2])
                copy.start()
                copies.append(copy)
    for copy in copies:
        copy.wait()


def params(megabytes):
    return pltpu.CompilerParams(vmem_limit_bytes=megabytes * 2**20)


VM = pl.BlockSpec(memory_space=pltpu.VMEM)
HBM = pl.BlockSpec(memory_space=pltpu.HBM)


def carried_in(value, reverse):
    count = lax.axis_size("ctx")
    rows = value.shape[0] // count
    mine = lax.all_to_all(value.reshape(count, rows, HD), "ctx", 0, 0)
    summed = pl.pallas_call(
        lambda x, o: scan_kernel(reverse, x, o),
        out_shape=jax.ShapeDtypeStruct(mine.shape, F32),
        in_specs=[VM],
        out_specs=VM,
        compiler_params=params(2),
        name="suffix" if reverse else "prefix",
    )(mine)
    return lax.all_to_all(summed, "ctx", 0, 0).reshape(value.shape)


def tp_sum(x):
    n = lax.axis_size("tp")
    x = x + lax.ppermute(x, "tp", [(i, i ^ 1) for i in range(n)])
    others = [lax.ppermute(x, "tp", [(i, i ^ flip) for i in range(n)]) for flip in (4, 2, 6)]
    return x + others[0] + others[1] + others[2]


def local(queries, keys, values, gate, gain, out_grad):
    rows, width = queries.shape
    pairs = width // PAIR
    gain_row = gain.reshape(1, width)
    half_shape = jax.ShapeDtypeStruct((rows, width), BF16)
    state_shape = jax.ShapeDtypeStruct((width, HD), F32)
    half_buf = pltpu.VMEM((rows, width), BF16)
    column = pltpu.VMEM((rows, HD), F32)
    dma = pltpu.SemaphoreType.DMA

    own = pl.pallas_call(
        state_kernel, in_specs=[HBM, HBM], out_specs=VM, out_shape=state_shape,
        scratch_shapes=[half_buf, half_buf, dma((pairs,)), dma((pairs,))],
        compiler_params=params(60), name="state",
    )(keys, values)
    states = carried_in(own, False)

    mixed, sums = pl.pallas_call(
        forward_kernel,
        in_specs=[VM] * 7,
        out_specs=[VM, VM],
        out_shape=[
            jax.ShapeDtypeStruct((rows, width), F32),
            jax.ShapeDtypeStruct((2, rows), F32),
        ],
        scratch_shapes=[column, column],
        compiler_params=params(16), name="forward",
    )(queries, keys, values, states, gain_row, gate, out_grad)
    total = tp_sum(sums)

    output, gate_grad, mixed_grad, own_after = pl.pallas_call(
        norm_kernel,
        in_specs=[VM] * 6,
        out_specs=[HBM, HBM, VM, VM],
        out_shape=[half_shape, half_shape, half_shape, state_shape],
        scratch_shapes=[half_buf, half_buf, column, column, dma((2, pairs))],
        compiler_params=params(16), name="norm",
    )(total, mixed, gate, gain_row, out_grad, queries)
    after = carried_in(own_after, True)

    q_grad, k_grad, v_grad = pl.pallas_call(
        backward_kernel,
        in_specs=[VM] * 6,
        out_specs=[HBM, HBM, HBM],
        out_shape=[half_shape, half_shape, half_shape],
        scratch_shapes=[half_buf, half_buf, half_buf, dma((3, pairs))],
        compiler_params=params(16), name="backward",
    )(queries, keys, values, after, states, mixed_grad)
    return output, q_grad, k_grad, v_grad, gate_grad


def solution(mesh):
    wide = P("ctx", "tp")
    return jax.shard_map(
        local,
        mesh=mesh,
        in_specs=(wide, wide, wide, wide, P("tp"), wide),
        out_specs=(wide, wide, wide, wide, wide),
        check_vma=False,
    )
```

time: 134 us -> 119 us (0.89)
  local copies, waits for them, and re-layouts: 8.42 us -> 0.03 us
  Pallas kernels: 23.3 us -> 16.1 us
    unnamed x26 -> x12, local copies, waits for them, and re-layouts: 8.42 us -> 0.03 us
    pallas_call x2, Pallas kernels: 3.74 us -> 0.07 us  [carried_in(): pl.pallas_call(lambda x, o: scan_kernel(reverse, x, o), out_shape=jax.Sha...]
    pallas_call x4, Pallas kernels: 19.5 us -> 16 us  [the longest x1 6.82 us: local(): pl.pallas_call(backward_kernel, in_specs=[VM] * 6, out_specs=[HBM, HBM, H...]
    ppermute x3 -> x4, waiting for transfers between devices: 5.36 us -> 4.55 us  [the longest x3 3.39 us: tp_sum(): lax.ppermute(x, 'tp', [(i, i ^ flip) for i in range(n)])]
    ppermute x3 -> x4, starting transfers between devices: 4.53 us -> 4.79 us  [the longest x3 4.7 us: tp_sum(): lax.ppermute(x, 'tp', [(i, i ^ flip) for i in range(n)])]
  transfers between devices with their start and end apart: 3 -> 4, of which waited for: 3 -> 4; matrix products, arithmetic and copies ran while one was open for 0% -> 0% of each run, Pallas kernels for 0% -> 0%
where the time goes in v2:
time: 119 us; the launch traced here: 118 us
  blocking collectives  92.1 us (77%)
  Pallas kernels  16.1 us (14%)
  starting transfers between devices  4.79 us (4%)
  waiting for transfers between devices  4.55 us (4%)
    all_to_all x2, blocking collectives, carried_in(): mine = lax.all_to_all(value.reshape(count, rows, HD), 'ctx', 0, 0)  50.2 us
    all_to_all x2, blocking collectives, carried_in(): return lax.all_to_all(summed, 'ctx', 0, 0).reshape(value.shape)  41.9 us
    pallas_call x1, Pallas kernels, local(): pl.pallas_call(backward_kernel, in_specs=[VM] * 6, out_specs=[HBM, HBM, H...  6.82 us
    ppermute x3, starting transfers between devices, tp_sum(): lax.ppermute(x, 'tp', [(i, i ^ flip) for i in range(n)])  4.7 us
    ppermute x3, waiting for transfers between devices, tp_sum(): lax.ppermute(x, 'tp', [(i, i ^ flip) for i in range(n)])  3.39 us
    pallas_call x1, Pallas kernels, local(): pl.pallas_call(state_kernel, in_specs=[HBM, HBM], out_specs=VM, out_shape...  3.26 us
    pallas_call x1, Pallas kernels, local(): pl.pallas_call(forward_kernel, in_specs=[VM] * 7, out_specs=[VM, VM], out...  3.08 us
    pallas_call x1, Pallas kernels, local(): pl.pallas_call(norm_kernel, in_specs=[VM] * 6, out_specs=[HBM, HBM, VM, V...  2.84 us
  transfers between devices with their start and end apart: 4, of which 4 were waited for; matrix products, arithmetic and copies ran while one was open for 0% of the time, Pallas kernels for 0%

profile of v2, /device:TPU:32, one launch (start us, length us, event | category | flops | bytes accessed | tf_op | source)
XLA Modules:
  0.0 118.5 jit_solution(3235931580044679671)
XLA Ops:
  0.6 0.0 copy-start.3
  0.6 0.0 copy-start.4
  0.7 3.3 %state.1 = f32[1024,128]{1,0:T(8,128)} custom-call(bf16[512,1024]{1,0:T(8,128)(2,1)} %k_ref.5, bf16[512,1024]{1,0:T(8,128)(2,1)} %v_ref.5), custom_call_target="tpu_custom_call" | custom-call | tf_op jit(solution)/shard_map/state/pallas_call | solution.py:207
  3.9 0.0 copy-start
  3.9 0.0 copy-start.1
  3.9 0.0 copy-start.2
  4.0 0.0 copy-start.5
  4.0 29.2 %all_to_all.20.x = f32[32,32,128]{2,1,0:T(8,128)S(1)} all-to-all(f32[32,32,128]{2,1,0:T(8,128)} %bitcast.11), channel_id=1, replica_groups=mesh['ctx'=32,'tp'=8] {'ctx'}, dimensions={0} | all-to-all | bytes 1048576 | tf_op jit(solution)/shard_map/all_to_all | solution.py:178
  33.3 21.6 %all_to_all.21 = f32[32,32,128]{2,1,0:T(8,128)S(1)} all-to-all(f32[32,32,128]{2,1,0:T(8,128)S(1)} %prefix.1), channel_id=1, replica_groups=mesh['ctx'=32,'tp'=8] {'ctx'}, dimensions={0} | all-to-all | bytes 1048576 | tf_op jit(solution)/shard_map/all_to_all | solution.py:187
  54.9 0.0 copy-done.3
  54.9 0.0 copy-done.4
  54.9 0.0 copy-done
  54.9 0.0 copy-done.1
  54.9 0.0 copy-done.2
  54.9 0.0 copy-done.5
  54.9 3.1 %forward.1 = (f32[512,1024]{1,0:T(8,128)S(1)}, f32[2,512]{1,0:T(2,128)S(1)}) custom-call(bf16[512,1024]{1,0:T(8,128)(2,1)S(1)} %copy-done, bf16[512,1024]{1,0:T(8,128)(2,1)S(1)} %copy-done.1, bf16[512,1024]{1,0:T(8,128)(2,1)S(1)} %copy-done.2, f32[1024,128]{1,0:T(8,128)S(1)} %bitcast.5, f32[1,1024]{1,0:T(1,128)S(1)} %bitcast.9, ...), custom_call_target="tpu_custom_call" | custom-call | tf_op jit(solution)/shard_map/forward/pallas_call | solution.py:214
  58.0 0.1 collective-permute-start
  58.1 1.2 collective-permute-done
  59.2 2.8 %collective-permute-start.3 = (f32[2,512]{1,0:T(2,128)S(1)}, f32[2,512]{1,0:T(2,128)S(1)}, u32[]{:S(2)}, u32[]{:S(2)}) collective-permute-start(f32[2,512]{1,0:T(2,128)S(1)} %add.12), channel_id=1, source_target_pairs={{0,6},{1,7},{2,4},{3,5},{4,2},{5,3},{6,0},{7,1},{8,14},{9,15},{10,... | collective-permute-start | bytes 12296 | tf_op jit(solution)/shard_map/ppermute | solution.py:193
  62.0 0.2 collective-permute-start.2
  62.2 1.7 %collective-permute-start.1 = (f32[2,512]{1,0:T(2,128)S(1)}, f32[2,512]{1,0:T(2,128)S(1)}, u32[]{:S(2)}, u32[]{:S(2)}) collective-permute-start(f32[2,512]{1,0:T(2,128)S(1)} %add.12), channel_id=1, source_target_pairs={{0,4},{1,5},{2,6},{3,7},{4,0},{5,1},{6,2},{7,3},{8,12},{9,13},{10,... | collective-permute-start | bytes 12296 | tf_op jit(solution)/shard_map/ppermute | solution.py:193
  63.9 0.1 collective-permute-done.3
  64.1 1.5 %collective-permute-done.2 = f32[2,512]{1,0:T(2,128)S(1)} collective-permute-done((f32[2,512]{1,0:T(2,128)S(1)}, f32[2,512]{1,0:T(2,128)S(1)}, u32[]{:S(2)}, u32[]{:S(2)}) %collective-permute-start.2) | collective-permute-done | bytes 4128 | tf_op jit(solution)/shard_map/ppermute | solution.py:193
  65.6 1.7 %collective-permute-done.1 = f32[2,512]{1,0:T(2,128)S(1)} collective-permute-done((f32[2,512]{1,0:T(2,128)S(1)}, f32[2,512]{1,0:T(2,128)S(1)}, u32[]{:S(2)}, u32[]{:S(2)}) %collective-permute-start.1) | collective-permute-done | bytes 4128 | tf_op jit(solution)/shard_map/ppermute | solution.py:193
  67.3 2.8 %norm.1 = (bf16[512,1024]{1,0:T(8,128)(2,1)}, bf16[512,1024]{1,0:T(8,128)(2,1)}, bf16[512,1024]{1,0:T(8,128)(2,1)S(1)}, f32[1024,128]{1,0:T(8,128)S(1)}) custom-call(f32[2,512]{1,0:T(2,128)S(1)} %add_add_fusion.sums_ref, f32[512,1024]{1,0:T(8,128)S(1)} %get-tuple-element.15.mixed_ref, bf16[512,1024]{1,0:T(8,128)(2,1)S(1)} %copy-done.3, ...), custom_call_target="tpu_custom_call" | custom-call | tf_op jit(solution)/shard_map/norm/pallas_call | solution.py:227
  70.2 21.0 %all_to_all.22.x = f32[32,32,128]{2,1,0:T(8,128)S(1)} all-to-all(f32[32,32,128]{2,1,0:T(8,128)S(1)} %bitcast.8), channel_id=1, replica_groups=mesh['ctx'=32,'tp'=8] {'ctx'}, dimensions={0} | all-to-all | bytes 1048576 | tf_op jit(solution)/shard_map/all_to_all | solution.py:178
  91.2 20.3 %all_to_all.23 = f32[32,32,128]{2,1,0:T(8,128)S(1)} all-to-all(f32[32,32,128]{2,1,0:T(8,128)S(1)} %suffix.1), channel_id=1, replica_groups=mesh['ctx'=32,'tp'=8] {'ctx'}, dimensions={0} | all-to-all | bytes 1048576 | tf_op jit(solution)/shard_map/all_to_all | solution.py:187
  111.5 6.8 %backward.1 = (bf16[512,1024]{1,0:T(8,128)(2,1)}, bf16[512,1024]{1,0:T(8,128)(2,1)}, bf16[512,1024]{1,0:T(8,128)(2,1)}) custom-call(bf16[512,1024]{1,0:T(8,128)(2,1)S(1)} %copy-done, bf16[512,1024]{1,0:T(8,128)(2,1)S(1)} %copy-done.1, bf16[512,1024]{1,0:T(8,128)(2,1)S(1)} %copy-done.2, f32[1024,128]{1,0:T(8,128)S(1)} %bitcast.7, f32[1024,128]{1,0:T(8,128)S(1)} %bitcast.6, ...), custom_call_target="tpu_custom_call" | custom-call | tf_op jit(solution)/shard_map/backward/pallas_call | solution.py:237
  (4 shorter events, 0.1 us)
Async XLA Ops:
  0.6 54.2 %copy-start.3 = (bf16[512,1024]{1,0:T(8,128)(2,1)S(1)}, bf16[512,1024]{1,0:T(8,128)(2,1)}, u32[]{:S(2)}) copy-start(bf16[512,1024]{1,0:T(8,128)(2,1)} %gate_ref.3) | copy-start | bytes 3145732
  0.6 54.2 %copy-start.4 = (bf16[512,1024]{1,0:T(8,128)(2,1)S(1)}, bf16[512,1024]{1,0:T(8,128)(2,1)}, u32[]{:S(2)}) copy-start(bf16[512,1024]{1,0:T(8,128)(2,1)} %dy_ref.3) | copy-start | bytes 3145732
  3.9 50.9 %copy-start = (bf16[512,1024]{1,0:T(8,128)(2,1)S(1)}, bf16[512,1024]{1,0:T(8,128)(2,1)}, u32[]{:S(2)}) copy-start(bf16[512,1024]{1,0:T(8,128)(2,1)} %q_ref.5) | copy-start | bytes 3145732
  3.9 50.9 %copy-start.1 = (bf16[512,1024]{1,0:T(8,128)(2,1)S(1)}, bf16[512,1024]{1,0:T(8,128)(2,1)}, u32[]{:S(2)}) copy-start(bf16[512,1024]{1,0:T(8,128)(2,1)} %k_ref.5) | copy-start | bytes 3145732
  3.9 50.9 %copy-start.2 = (bf16[512,1024]{1,0:T(8,128)(2,1)S(1)}, bf16[512,1024]{1,0:T(8,128)(2,1)}, u32[]{:S(2)}) copy-start(bf16[512,1024]{1,0:T(8,128)(2,1)} %v_ref.5) | copy-start | bytes 3145732
  4.0 50.9 %copy-start.5 = (f32[1024]{0:T(1024)S(1)}, f32[1024]{0:T(1024)}, u32[]{:S(2)}) copy-start(f32[1024]{0:T(1024)} %param.10) | copy-start | bytes 12292
  58.0 1.3 %collective-permute-start = (f32[2,512]{1,0:T(2,128)S(1)}, f32[2,512]{1,0:T(2,128)S(1)}, u32[]{:S(2)}, u32[]{:S(2)}) collective-permute-start(f32[2,512]{1,0:T(2,128)S(1)} %get-tuple-element.14), channel_id=1, source_target_pairs={{0,1},{1,0},{2,3},{3,2},{4,5},{5,4},{6,7},{7,6},{8,9},{9,8},{10,11... | collective-permute-start | bytes 12296 | tf_op jit(solution)/shard_map/ppermute | solution.py:192
  59.2 4.8 %collective-permute-start.3 = (f32[2,512]{1,0:T(2,128)S(1)}, f32[2,512]{1,0:T(2,128)S(1)}, u32[]{:S(2)}, u32[]{:S(2)}) collective-permute-start(f32[2,512]{1,0:T(2,128)S(1)} %add.12), channel_id=1, source_target_pairs={{0,6},{1,7},{2,4},{3,5},{4,2},{5,3},{6,0},{7,1},{8,14},{9,15},{10,... | collective-permute-start | bytes 12296 | tf_op jit(solution)/shard_map/ppermute | solution.py:193
  62.0 3.6 %collective-permute-start.2 = (f32[2,512]{1,0:T(2,128)S(1)}, f32[2,512]{1,0:T(2,128)S(1)}, u32[]{:S(2)}, u32[]{:S(2)}) collective-permute-start(f32[2,512]{1,0:T(2,128)S(1)} %add.12), channel_id=1, source_target_pairs={{0,2},{1,3},{2,0},{3,1},{4,6},{5,7},{6,4},{7,5},{8,10},{9,11},{10,... | collective-permute-start | bytes 12296 | tf_op jit(solution)/shard_map/ppermute | solution.py:193
  62.2 5.1 %collective-permute-start.1 = (f32[2,512]{1,0:T(2,128)S(1)}, f32[2,512]{1,0:T(2,128)S(1)}, u32[]{:S(2)}, u32[]{:S(2)}) collective-permute-start(f32[2,512]{1,0:T(2,128)S(1)} %add.12), channel_id=1, source_target_pairs={{0,4},{1,5},{2,6},{3,7},{4,0},{5,1},{6,2},{7,3},{8,12},{9,13},{10,... | collective-permute-start | bytes 12296 | tf_op jit(solution)/shard_map/ppermute | solution.py:193

commit v3 on v2

--- a/solution.py
+++ b/solution.py
@@ -41,25 +41,10 @@
     return jnp.where(cols <= rows, x, 0.0)
 
 
-def fetch(source, target, sems, width):
-    copies = []
-    for i in range(source.shape[1] // width):
-        cols = pl.ds(i * width, width)
-        copy = pltpu.make_async_copy(source.at[:, cols], target.at[:, cols], sems.at[i])
-        copy.start()
-        copies.append(copy)
-    return copies
-
-
-def state_kernel(k_ref, v_ref, out_ref, k_buf, v_buf, k_sem, v_sem):
-    k_copies = fetch(k_ref, k_buf, k_sem, PAIR)
-    v_copies = fetch(v_ref, v_buf, v_sem, PAIR)
-    for i in range(len(k_copies)):
-        k_copies[i].wait()
-        v_copies[i].wait()
-        for h in (2 * i, 2 * i + 1):
-            cols = slice(h * HD, (h + 1) * HD)
-            out_ref[cols, :] = tn(k_buf[:, cols], v_buf[:, cols])
+def state_kernel(k_ref, v_ref, out_ref):
+    for h in range(k_ref.shape[1] // HD):
+        cols = slice(h * HD, (h + 1) * HD)
+        out_ref[cols, :] = tn(k_ref[:, cols], v_ref[:, cols])
 
 
 def scan_kernel(reverse, x_ref, out_ref):
@@ -97,10 +82,10 @@
     sums_ref[1:2, :] = jnp.sum(cross[...].T, axis=0, keepdims=True)
 
 
-def norm_kernel(sums_ref, mixed_ref, gate_ref, gain_ref, dy_ref, q_ref,
+def norm_kernel(sums0_ref, sums1_ref, sums2_ref, sums3_ref, mixed_ref, gate_ref, gain_ref, dy_ref, q_ref,
                 out_ref, ggrad_ref, d_ref, g_ref,
                 out_buf, ggrad_buf, inv_ref, proj_ref, sems):
-    total = sums_ref[...]
+    total = (sums0_ref[...] + sums1_ref[...]) + (sums2_ref[...] + sums3_ref[...])
     inv = lax.rsqrt(total[0:1] / D + EPS)
     proj = inv * (total[1:2] / D)
     inv_ref[...] = jnp.broadcast_to(inv, (HD, inv.shape[1])).T
@@ -129,8 +114,8 @@
         copy.wait()
 
 
-def backward_kernel(q_ref, k_ref, v_ref, after_ref, s_ref, d_ref,
-                    qg_ref, kg_ref, vg_ref, qg_buf, kg_buf, vg_buf, sems):
+def partial_kernel(q_ref, k_ref, v_ref, s_ref, d_ref, qg_ref, parts_ref, qg_buf, sems):
+    rows = q_ref.shape[0]
     copies = []
     for h in range(q_ref.shape[1] // HD):
         cols = slice(h * HD, (h + 1) * HD)
@@ -142,26 +127,45 @@
         a00 = causal_tile(nt(q0, k[:HALF])).astype(BF16)
         a10 = nt(q1, k[:HALF]).astype(BF16)
         a11 = causal_tile(nt(q1, k[HALF:])).astype(BF16)
-        after_high, after_low = halves(after_ref[cols, :])
-        after_wide = jnp.concatenate([after_high, after_low], 1)
-        after_tall = jnp.concatenate([after_high, after_low], 0)
         q_inter = nt(jnp.concatenate([d, d], 1), jnp.concatenate(halves(s_ref[cols, :]), 1))
-        k_inter = nt(jnp.concatenate([v, v], 1), after_wide)
-        v_inter = nn(jnp.concatenate([k, k], 1), after_tall)
         qg_buf[:HALF, cols] = (nn(p00, k[:HALF]) + q_inter[:HALF]).astype(BF16)
         qg_buf[HALF:, cols] = (nn(p10, k[:HALF]) + nn(p11, k[HALF:]) + q_inter[HALF:]).astype(BF16)
-        kg_buf[:HALF, cols] = (tn(p00, q0) + tn(p10, q1) + k_inter[:HALF]).astype(BF16)
-        kg_buf[HALF:, cols] = (tn(p11, q1) + k_inter[HALF:]).astype(BF16)
-        vg_buf[:HALF, cols] = (tn(a00, d0) + tn(a10, d1) + v_inter[:HALF]).astype(BF16)
-        vg_buf[HALF:, cols] = (tn(a11, d1) + v_inter[HALF:]).astype(BF16)
+        parts_ref[:HALF, cols] = (tn(p00, q0) + tn(p10, q1)).astype(BF16)
+        parts_ref[HALF:rows, cols] = (tn(p11, q1)).astype(BF16)
+        parts_ref[rows : rows + HALF, cols] = (tn(a00, d0) + tn(a10, d1)).astype(BF16)
+        parts_ref[rows + HALF :, cols] = (tn(a11, d1)).astype(BF16)
         if h % 2 == 1:
             both = pl.ds((h - 1) * HD, PAIR)
-            for j, (buf, ref) in enumerate(((qg_buf, qg_ref), (kg_buf, kg_ref), (vg_buf, vg_ref))):
+            copy = pltpu.make_async_copy(qg_buf.at[:, both], qg_ref.at[:, both], sems.at[h // 2])
+            copy.start()
+            copies.append(copy)
+    for copy in copies:
+        copy.wait()
+
+
+def gradient_kernel(k_ref, v_ref, after_ref, parts_ref, kg_ref, vg_ref, kg_buf, vg_buf, sems):
+    rows = k_ref.shape[0]
+    copies = []
+    for h in range(k_ref.shape[1] // HD):
+        cols = slice(h * HD, (h + 1) * HD)
+        k, v = k_ref[:, cols], v_ref[:, cols]
+        after_high, after_low = halves(after_ref[cols, :])
+        k_inter = nt(jnp.concatenate([v, v], 1), jnp.concatenate([after_high, after_low], 1))
+        v_inter = nn(jnp.concatenate([k, k], 1), jnp.concatenate([after_high, after_low], 0))
+        kg_buf[:, cols] = (parts_ref[:rows, cols] + k_inter).astype(BF16)
+        vg_buf[:, cols] = (parts_ref[rows:, cols] + v_inter).astype(BF16)
+        if h % 2 == 1:
+            both = pl.ds((h - 1) * HD, PAIR)
+            for j, (buf, ref) in enumerate(((kg_buf, kg_ref), (vg_buf, vg_ref))):
                 copy = pltpu.make_async_copy(buf.at[:, both], ref.at[:, both], sems.at[j, h // 2])
                 copy.start()
                 copies.append(copy)
     for copy in copies:
         copy.wait()
+
+
+def cost(flops, moved):
+    return pl.CostEstimate(flops=flops, bytes_accessed=moved, transcendentals=0)
 
 
 def params(megabytes):
@@ -187,11 +191,10 @@
     return lax.all_to_all(summed, "ctx", 0, 0).reshape(value.shape)
 
 
-def tp_sum(x):
+def tp_parts(x):
     n = lax.axis_size("tp")
     x = x + lax.ppermute(x, "tp", [(i, i ^ 1) for i in range(n)])
-    others = [lax.ppermute(x, "tp", [(i, i ^ flip) for i in range(n)]) for flip in (4, 2, 6)]
-    return x + others[0] + others[1] + others[2]
+    return [x] + [lax.ppermute(x, "tp", [(i, i ^ flip) for i in range(n)]) for flip in (4, 2, 6)]
 
 
 def local(queries, keys, values, gate, gain, out_grad):
@@ -199,15 +202,15 @@
     pairs = width // PAIR
     gain_row = gain.reshape(1, width)
     half_shape = jax.ShapeDtypeStruct((rows, width), BF16)
+    double_shape = jax.ShapeDtypeStruct((2 * rows, width), BF16)
     state_shape = jax.ShapeDtypeStruct((width, HD), F32)
     half_buf = pltpu.VMEM((rows, width), BF16)
     column = pltpu.VMEM((rows, HD), F32)
     dma = pltpu.SemaphoreType.DMA
 
     own = pl.pallas_call(
-        state_kernel, in_specs=[HBM, HBM], out_specs=VM, out_shape=state_shape,
-        scratch_shapes=[half_buf, half_buf, dma((pairs,)), dma((pairs,))],
-        compiler_params=params(60), name="state",
+        state_kernel, in_specs=[VM, VM], out_specs=VM, out_shape=state_shape,
+        compiler_params=params(8), name="state",
     )(keys, values)
     states = carried_in(own, False)
 
@@ -222,26 +225,33 @@
         scratch_shapes=[column, column],
         compiler_params=params(16), name="forward",
     )(queries, keys, values, states, gain_row, gate, out_grad)
-    total = tp_sum(sums)
 
     output, gate_grad, mixed_grad, own_after = pl.pallas_call(
         norm_kernel,
-        in_specs=[VM] * 6,
+        in_specs=[VM] * 9,
         out_specs=[HBM, HBM, VM, VM],
         out_shape=[half_shape, half_shape, half_shape, state_shape],
         scratch_shapes=[half_buf, half_buf, column, column, dma((2, pairs))],
         compiler_params=params(16), name="norm",
-    )(total, mixed, gate, gain_row, out_grad, queries)
+    )(*tp_parts(sums), mixed, gate, gain_row, out_grad, queries)
     after = carried_in(own_after, True)
 
-    q_grad, k_grad, v_grad = pl.pallas_call(
-        backward_kernel,
-        in_specs=[VM] * 6,
-        out_specs=[HBM, HBM, HBM],
-        out_shape=[half_shape, half_shape, half_shape],
-        scratch_shapes=[half_buf, half_buf, half_buf, dma((3, pairs))],
-        compiler_params=params(16), name="backward",
-    )(queries, keys, values, after, states, mixed_grad)
+    q_grad, parts = pl.pallas_call(
+        partial_kernel,
+        in_specs=[VM] * 5,
+        out_specs=[HBM, VM],
+        out_shape=[half_shape, double_shape],
+        scratch_shapes=[half_buf, dma((pairs,))],
+        compiler_params=params(16), cost_estimate=cost(5 * 10**9, 10 * 2**20), name="partial",
+    )(queries, keys, values, states, mixed_grad)
+    k_grad, v_grad = pl.pallas_call(
+        gradient_kernel,
+        in_specs=[VM] * 4,
+        out_specs=[HBM, HBM],
+        out_shape=[half_shape, half_shape],
+        scratch_shapes=[half_buf, half_buf, dma((2, pairs))],
+        compiler_params=params(16), name="gradient",
+    )(keys, values, after, parts)
     return output, q_grad, k_grad, v_grad, gate_grad
 
 

time: 119 us -> 118 us (level)
  blocking collectives: 92.1 us -> 71.6 us
  local copies, waits for them, and re-layouts: 0.03 us -> 8.46 us
  waiting for transfers between devices: 4.55 us -> 11.3 us
  starting transfers between devices: 4.79 us -> 9.7 us
    all_to_all x2 -> x1, blocking collectives: 41.9 us -> 21.6 us  [carried_in(): return lax.all_to_all(summed, 'ctx', 0, 0).reshape(value.shape)]
    unnamed x12 -> x30, local copies, waits for them, and re-layouts: 0.03 us -> 8.46 us
    all_to_all x0 -> x1, waiting for transfers between devices: none -> 6.71 us  [carried_in(): return lax.all_to_all(summed, 'ctx', 0, 0).reshape(value.shape)]
    all_to_all x0 -> x1, starting transfers between devices: none -> 4.91 us  [carried_in(): return lax.all_to_all(summed, 'ctx', 0, 0).reshape(value.shape)]
    pallas_call x3 -> x4, Pallas kernels: 12.9 us -> 11.8 us  [the longest x1 5.37 us: local(): pl.pallas_call(partial_kernel, in_specs=[VM] * 5, out_specs=[HBM, VM], ou...]
  transfers between devices with their start and end apart: 4 -> 5, of which waited for: 4 -> 5; matrix products, arithmetic and copies ran while one was open for 0% -> 0% of each run, Pallas kernels for 0% -> 5%
where the time goes in v3:
time: 118 us; the launch traced here: 117 us
  blocking collectives  71.6 us (61%)
  Pallas kernels  15 us (13%)
  waiting for transfers between devices  11.3 us (10%)
  starting transfers between devices  9.7 us (8%)
  local copies, waits for them, and re-layouts  8.46 us (7%)
    all_to_all x2, blocking collectives, carried_in(): mine = lax.all_to_all(value.reshape(count, rows, HD), 'ctx', 0, 0)  50 us
    all_to_all x1, blocking collectives, carried_in(): return lax.all_to_all(summed, 'ctx', 0, 0).reshape(value.shape)  21.6 us
    unnamed x30, local copies, waits for them, and re-layouts  8.46 us
    all_to_all x1, waiting for transfers between devices, carried_in(): return lax.all_to_all(summed, 'ctx', 0, 0).reshape(value.shape)  6.71 us
    pallas_call x1, Pallas kernels, local(): pl.pallas_call(partial_kernel, in_specs=[VM] * 5, out_specs=[HBM, VM], ou...  5.37 us
    all_to_all x1, starting transfers between devices, carried_in(): return lax.all_to_all(summed, 'ctx', 0, 0).reshape(value.shape)  4.91 us
    ppermute x3, starting transfers between devices, tp_parts(): lax.ppermute(x, 'tp', [(i, i ^ flip) for i in range(n)])  4.7 us
    ppermute x3, waiting for transfers between devices, tp_parts(): lax.ppermute(x, 'tp', [(i, i ^ flip) for i in range(n)])  3.41 us
  transfers between devices with their start and end apart: 5, of which 5 were waited for; matrix products, arithmetic and copies ran while one was open for 0% of the time, Pallas kernels for 5%

profile of v3, /device:TPU:32, one launch (start us, length us, event | category | flops | bytes accessed | tf_op | source)
XLA Modules:
  0.0 117.0 jit_solution(12827039905324411171)
XLA Ops:
  0.6 0.0 copy-start
  0.6 1.2 %copy-done = bf16[512,1024]{1,0:T(8,128)(2,1)S(1)} copy-done((bf16[512,1024]{1,0:T(8,128)(2,1)S(1)}, bf16[512,1024]{1,0:T(8,128)(2,1)}, u32[]{:S(2)}) %copy-start) | copy-done | bytes 1048600
  1.9 1.2 %copy-done.2 = bf16[512,1024]{1,0:T(8,128)(2,1)S(1)} copy-done((bf16[512,1024]{1,0:T(8,128)(2,1)S(1)}, bf16[512,1024]{1,0:T(8,128)(2,1)}, u32[]{:S(2)}) %copy-start.2) | copy-done | bytes 1048600
  3.1 0.5 state.1
  3.6 0.0 copy-start.1
  3.6 0.0 copy-start.3
  3.6 0.0 copy-start.4
  3.6 0.0 copy-start.12
  3.7 29.0 %all_to_all.20.x = f32[32,32,128]{2,1,0:T(8,128)S(1)} all-to-all(f32[32,32,128]{2,1,0:T(8,128)S(1)} %bitcast.7), channel_id=1, replica_groups=mesh['ctx'=32,'tp'=8] {'ctx'}, dimensions={0} | all-to-all | bytes 1048576 | tf_op jit(solution)/shard_map/all_to_all | solution.py:182
  32.7 21.6 %all_to_all.21 = f32[32,32,128]{2,1,0:T(8,128)S(1)} all-to-all(f32[32,32,128]{2,1,0:T(8,128)S(1)} %prefix.1), channel_id=1, replica_groups=mesh['ctx'=32,'tp'=8] {'ctx'}, dimensions={0} | all-to-all | bytes 1048576 | tf_op jit(solution)/shard_map/all_to_all | solution.py:191
  54.4 3.1 %forward.1 = (f32[512,1024]{1,0:T(8,128)S(1)}, f32[2,512]{1,0:T(2,128)S(1)}) custom-call(bf16[512,1024]{1,0:T(8,128)(2,1)S(1)} %copy-done.6, bf16[512,1024]{1,0:T(8,128)(2,1)S(1)} %copy-done.1, bf16[512,1024]{1,0:T(8,128)(2,1)S(1)} %copy-done.3, f32[1024,128]{1,0:T(8,128)S(1)} %bitcast.5, f32[1,1024]{1,0:T(1,128)S(1)} %bitcast.9, ...), custom_call_target="tpu_custom_call" | custom-call | tf_op jit(solution)/shard_map/forward/pallas_call | solution.py:217
  57.5 0.1 collective-permute-start
  57.6 1.2 collective-permute-done
  58.7 2.8 %collective-permute-start.3 = (f32[2,512]{1,0:T(2,128)S(1)}, f32[2,512]{1,0:T(2,128)S(1)}, u32[]{:S(2)}, u32[]{:S(2)}) collective-permute-start(f32[2,512]{1,0:T(2,128)S(1)} %add.3.sums0_ref), channel_id=1, source_target_pairs={{0,6},{1,7},{2,4},{3,5},{4,2},{5,3},{6,0},{7,1},{8,14},{9,15},{10,... | collective-permute-start | bytes 12296 | tf_op jit(solution)/shard_map/ppermute | solution.py:197
  61.5 0.2 collective-permute-start.2
  61.7 1.7 %collective-permute-start.1 = (f32[2,512]{1,0:T(2,128)S(1)}, f32[2,512]{1,0:T(2,128)S(1)}, u32[]{:S(2)}, u32[]{:S(2)}) collective-permute-start(f32[2,512]{1,0:T(2,128)S(1)} %add.3.sums0_ref), channel_id=1, source_target_pairs={{0,4},{1,5},{2,6},{3,7},{4,0},{5,1},{6,2},{7,3},{8,12},{9,13},{10,... | collective-permute-start | bytes 12296 | tf_op jit(solution)/shard_map/ppermute | solution.py:197
  63.4 0.1 collective-permute-done.3.sums3_ref
  63.6 1.5 %collective-permute-done.2.sums2_ref = f32[2,512]{1,0:T(2,128)S(1)} collective-permute-done((f32[2,512]{1,0:T(2,128)S(1)}, f32[2,512]{1,0:T(2,128)S(1)}, u32[]{:S(2)}, u32[]{:S(2)}) %collective-permute-start.2) | collective-permute-done | bytes 4128 | tf_op jit(solution)/shard_map/ppermute | solution.py:197
  65.1 1.7 %collective-permute-done.1.sums1_ref = f32[2,512]{1,0:T(2,128)S(1)} collective-permute-done((f32[2,512]{1,0:T(2,128)S(1)}, f32[2,512]{1,0:T(2,128)S(1)}, u32[]{:S(2)}, u32[]{:S(2)}) %collective-permute-start.1) | collective-permute-done | bytes 4128 | tf_op jit(solution)/shard_map/ppermute | solution.py:197
  66.9 2.8 %norm.1 = (bf16[512,1024]{1,0:T(8,128)(2,1)}, bf16[512,1024]{1,0:T(8,128)(2,1)}, bf16[512,1024]{1,0:T(8,128)(2,1)S(1)}, f32[1024,128]{1,0:T(8,128)S(1)}) custom-call(f32[2,512]{1,0:T(2,128)S(1)} %add.3.sums0_ref, f32[2,512]{1,0:T(2,128)S(1)} %collective-permute-done.1.sums1_ref, f32[2,512]{1,0:T(2,128)S(1)} %collective-permute-done.2.sums2_ref, ...), custom_call_target="tpu_custom_call" | custom-call | tf_op jit(solution)/shard_map/norm/pallas_call | solution.py:229
  69.6 0.0 copy-start.13
  69.6 21.0 %all_to_all.22.x = f32[32,32,128]{2,1,0:T(8,128)S(1)} all-to-all(f32[32,32,128]{2,1,0:T(8,128)S(1)} %bitcast.8), channel_id=1, replica_groups=mesh['ctx'=32,'tp'=8] {'ctx'}, dimensions={0} | all-to-all | bytes 1048576 | tf_op jit(solution)/shard_map/all_to_all | solution.py:182
  90.7 0.8 copy-done.11
  91.5 4.9 %all-to-all-start.3 = ((f32[32,32,128]{2,1,0:T(8,128)}), f32[32,32,128]{2,1,0:T(8,128)}, u32[]{:S(2)}, u32[]{:S(2)}) async-start(f32[32,32,128]{2,1,0:T(8,128)} %copy-done.11), calls=%async_computation.3 | async-start | bytes 1048576 | tf_op jit(solution)/shard_map/all_to_all | solution.py:191
  96.4 0.0 copy-start.8
  96.4 1.0 copy-done.8
  97.4 1.2 %copy-done.14 = bf16[512,1024]{1,0:T(8,128)(2,1)S(1)} copy-done((bf16[512,1024]{1,0:T(8,128)(2,1)S(1)}, bf16[512,1024]{1,0:T(8,128)(2,1)}, u32[]{:S(2)}) %copy-start.14) | copy-done | bytes 1048600
  98.6 5.4 %partial.1 = (bf16[512,1024]{1,0:T(8,128)(2,1)}, bf16[1024,1024]{1,0:T(8,128)(2,1)S(1)}) custom-call(bf16[512,1024]{1,0:T(8,128)(2,1)S(1)} %copy-done.6, bf16[512,1024]{1,0:T(8,128)(2,1)S(1)} %copy-done.1, bf16[512,1024]{1,0:T(8,128)(2,1)S(1)} %copy-done.3, f32[1024,128]{1,0:T(8,128)S(1)} %bitcast.6, bf16[512,1024]{1,0:T(8,128)(2,1)S(1)} %copy-done.14), custom_call_target="tpu_custom_call" | custom-call | flops 5000000000 | bytes 10485760 | tf_op jit(solution)/shard_map/partial/pallas_call | solution.py:239
  104.0 1.3 %copy-done.9 = bf16[1024,1024]{1,0:T(8,128)(2,1)} copy-done((bf16[1024,1024]{1,0:T(8,128)(2,1)}, bf16[1024,1024]{1,0:T(8,128)(2,1)S(1)}, u32[]{:S(2)}) %copy-start.9) | copy-done | bytes 2097176
  105.4 6.7 %all-to-all-done.3 = f32[32,32,128]{2,1,0:T(8,128)} async-done(((f32[32,32,128]{2,1,0:T(8,128)}), f32[32,32,128]{2,1,0:T(8,128)}, u32[]{:S(2)}, u32[]{:S(2)}) %all-to-all-start.3) | async-done | bytes 524320 | tf_op jit(solution)/shard_map/all_to_all | solution.py:191
  112.1 1.6 %copy-done.10 = bf16[1024,1024]{1,0:T(8,128)(2,1)S(1)} copy-done((bf16[1024,1024]{1,0:T(8,128)(2,1)S(1)}, bf16[1024,1024]{1,0:T(8,128)(2,1)}, u32[]{:S(2)}) %copy-start.10) | copy-done | bytes 2097176
  113.7 3.2 %gradient.1 = (bf16[512,1024]{1,0:T(8,128)(2,1)}, bf16[512,1024]{1,0:T(8,128)(2,1)}) custom-call(bf16[512,1024]{1,0:T(8,128)(2,1)S(1)} %copy-done.1, bf16[512,1024]{1,0:T(8,128)(2,1)S(1)} %copy-done.3, f32[1024,128]{1,0:T(8,128)} %bitcast.4.after_ref, bf16[1024,1024]{1,0:T(8,128)(2,1)S(1)} %copy-done.10), custom_call_target="tpu_custom_call" | custom-call | tf_op jit(solution)/shard_map/gradient/pallas_call | solution.py:247
  (19 shorter events, 0.1 us)
Async XLA Ops:
  0.6 1.2 %copy-start = (bf16[512,1024]{1,0:T(8,128)(2,1)S(1)}, bf16[512,1024]{1,0:T(8,128)(2,1)}, u32[]{:S(2)}) copy-start(bf16[512,1024]{1,0:T(8,128)(2,1)} %k_ref.7) | copy-start | bytes 3145732
  1.9 1.2 %copy-start.2 = (bf16[512,1024]{1,0:T(8,128)(2,1)S(1)}, bf16[512,1024]{1,0:T(8,128)(2,1)}, u32[]{:S(2)}) copy-start(bf16[512,1024]{1,0:T(8,128)(2,1)} %v_ref.7) | copy-start | bytes 3145732
  3.1 51.2 %copy-start.5 = (bf16[512,1024]{1,0:T(8,128)(2,1)S(1)}, bf16[512,1024]{1,0:T(8,128)(2,1)}, u32[]{:S(2)}) copy-start(bf16[512,1024]{1,0:T(8,128)(2,1)} %dy_ref.3) | copy-start | bytes 3145732
  3.1 51.2 %copy-start.6 = (bf16[512,1024]{1,0:T(8,128)(2,1)S(1)}, bf16[512,1024]{1,0:T(8,128)(2,1)}, u32[]{:S(2)}) copy-start(bf16[512,1024]{1,0:T(8,128)(2,1)} %q_ref.5) | copy-start | bytes 3145732
  3.6 50.7 %copy-start.1 = (bf16[512,1024]{1,0:T(8,128)(2,1)S(1)}, bf16[512,1024]{1,0:T(8,128)(2,1)}, u32[]{:S(2)}) copy-start(bf16[512,1024]{1,0:T(8,128)(2,1)} %k_ref.7) | copy-start | bytes 3145732
  3.6 50.7 %copy-start.3 = (bf16[512,1024]{1,0:T(8,128)(2,1)S(1)}, bf16[512,1024]{1,0:T(8,128)(2,1)}, u32[]{:S(2)}) copy-start(bf16[512,1024]{1,0:T(8,128)(2,1)} %v_ref.7) | copy-start | bytes 3145732
  3.6 50.7 %copy-start.4 = (bf16[512,1024]{1,0:T(8,128)(2,1)S(1)}, bf16[512,1024]{1,0:T(8,128)(2,1)}, u32[]{:S(2)}) copy-start(bf16[512,1024]{1,0:T(8,128)(2,1)} %gate_ref.3) | copy-start | bytes 3145732
  3.6 50.7 %copy-start.12 = (f32[1024]{0:T(1024)S(1)}, f32[1024]{0:T(1024)}, u32[]{:S(2)}) copy-start(f32[1024]{0:T(1024)} %param.10) | copy-start | bytes 12292
  54.3 3.2 %copy-start.7 = (f32[32,32,128]{2,1,0:T(8,128)}, f32[32,32,128]{2,1,0:T(8,128)S(1)}, u32[]{:S(2)}) copy-start(f32[32,32,128]{2,1,0:T(8,128)S(1)} %all_to_all.21) | copy-start | bytes 1572868
  57.5 1.3 %collective-permute-start = (f32[2,512]{1,0:T(2,128)S(1)}, f32[2,512]{1,0:T(2,128)S(1)}, u32[]{:S(2)}, u32[]{:S(2)}) collective-permute-start(f32[2,512]{1,0:T(2,128)S(1)} %get-tuple-element.15), channel_id=1, source_target_pairs={{0,1},{1,0},{2,3},{3,2},{4,5},{5,4},{6,7},{7,6},{8,9},{9,8},{10,11... | collective-permute-start | bytes 12296 | tf_op jit(solution)/shard_map/ppermute | solution.py:196
  58.7 4.8 %collective-permute-start.3 = (f32[2,512]{1,0:T(2,128)S(1)}, f32[2,512]{1,0:T(2,128)S(1)}, u32[]{:S(2)}, u32[]{:S(2)}) collective-permute-start(f32[2,512]{1,0:T(2,128)S(1)} %add.3.sums0_ref), channel_id=1, source_target_pairs={{0,6},{1,7},{2,4},{3,5},{4,2},{5,3},{6,0},{7,1},{8,14},{9,15},{10,... | collective-permute-start | bytes 12296 | tf_op jit(solution)/shard_map/ppermute | solution.py:197
  61.5 3.6 %collective-permute-start.2 = (f32[2,512]{1,0:T(2,128)S(1)}, f32[2,512]{1,0:T(2,128)S(1)}, u32[]{:S(2)}, u32[]{:S(2)}) collective-permute-start(f32[2,512]{1,0:T(2,128)S(1)} %add.3.sums0_ref), channel_id=1, source_target_pairs={{0,2},{1,3},{2,0},{3,1},{4,6},{5,7},{6,4},{7,5},{8,10},{9,11},{10,... | collective-permute-start | bytes 12296 | tf_op jit(solution)/shard_map/ppermute | solution.py:197
  61.7 5.1 %collective-permute-start.1 = (f32[2,512]{1,0:T(2,128)S(1)}, f32[2,512]{1,0:T(2,128)S(1)}, u32[]{:S(2)}, u32[]{:S(2)}) collective-permute-start(f32[2,512]{1,0:T(2,128)S(1)} %add.3.sums0_ref), channel_id=1, source_target_pairs={{0,4},{1,5},{2,6},{3,7},{4,0},{5,1},{6,2},{7,3},{8,12},{9,13},{10,... | collective-permute-start | bytes 12296 | tf_op jit(solution)/shard_map/ppermute | solution.py:197
  69.6 21.0 %copy-start.13 = (bf16[512,1024]{1,0:T(8,128)(2,1)}, bf16[512,1024]{1,0:T(8,128)(2,1)S(1)}, u32[]{:S(2)}) copy-start(bf16[512,1024]{1,0:T(8,128)(2,1)S(1)} %get-tuple-element.18.d_ref) | copy-start | bytes 3145732
  90.7 0.8 copy-start.11
  91.5 20.6 %all-to-all-start.3 = ((f32[32,32,128]{2,1,0:T(8,128)}), f32[32,32,128]{2,1,0:T(8,128)}, u32[]{:S(2)}, u32[]{:S(2)}) async-start(f32[32,32,128]{2,1,0:T(8,128)} %copy-done.11), calls=%async_computation.3 | async-start | bytes 1048576 | tf_op jit(solution)/shard_map/all_to_all | solution.py:191
  96.4 1.0 copy-start.8
  97.4 1.2 %copy-start.14 = (bf16[512,1024]{1,0:T(8,128)(2,1)S(1)}, bf16[512,1024]{1,0:T(8,128)(2,1)}, u32[]{:S(2)}) copy-start(bf16[512,1024]{1,0:T(8,128)(2,1)} %copy-done.13) | copy-start | bytes 3145732
  104.0 1.3 %copy-start.9 = (bf16[1024,1024]{1,0:T(8,128)(2,1)}, bf16[1024,1024]{1,0:T(8,128)(2,1)S(1)}, u32[]{:S(2)}) copy-start(bf16[1024,1024]{1,0:T(8,128)(2,1)S(1)} %get-tuple-element.21.parts_ref) | copy-start | bytes 6291460
  112.1 1.6 %copy-start.10 = (bf16[1024,1024]{1,0:T(8,128)(2,1)S(1)}, bf16[1024,1024]{1,0:T(8,128)(2,1)}, u32[]{:S(2)}) copy-start(bf16[1024,1024]{1,0:T(8,128)(2,1)} %copy-done.9) | copy-start | bytes 6291460

commit v4 on v3

--- a/solution.py
+++ b/solution.py
@@ -83,27 +83,33 @@
 
 
 def norm_kernel(sums0_ref, sums1_ref, sums2_ref, sums3_ref, mixed_ref, gate_ref, gain_ref, dy_ref, q_ref,
-                out_ref, ggrad_ref, d_ref, g_ref,
-                out_buf, ggrad_buf, inv_ref, proj_ref, sems):
+                d_ref, g_ref, inv_ref, proj_ref):
     total = (sums0_ref[...] + sums1_ref[...]) + (sums2_ref[...] + sums3_ref[...])
     inv = lax.rsqrt(total[0:1] / D + EPS)
     proj = inv * (total[1:2] / D)
     inv_ref[...] = jnp.broadcast_to(inv, (HD, inv.shape[1])).T
     proj_ref[...] = jnp.broadcast_to(proj, (HD, proj.shape[1])).T
-    copies = []
     for h in range(q_ref.shape[1] // HD):
         cols = slice(h * HD, (h + 1) * HD)
-        inv, proj = inv_ref[...], proj_ref[...]
+        inv = inv_ref[...]
         sig = jax.nn.sigmoid(gate_ref[:, cols].astype(F32))
-        gain = gain_ref[:, cols]
-        gain_sig = gain * sig
-        dn = dy_ref[:, cols].astype(F32) * gain_sig
+        dn = dy_ref[:, cols].astype(F32) * (gain_ref[:, cols] * sig)
         normed = mixed_ref[:, cols] * inv
-        out_buf[:, cols] = (normed * gain_sig).astype(BF16)
-        grad = (inv * (dn - normed * proj)).astype(BF16)
-        ggrad_buf[:, cols] = (dn * normed * (1.0 - sig)).astype(BF16)
+        grad = (inv * (dn - normed * proj_ref[...])).astype(BF16)
         d_ref[:, cols] = grad
         g_ref[cols, :] = tn(q_ref[:, cols], grad)
+
+
+def output_kernel(mixed_ref, inv_ref, gate_ref, gain_ref, dy_ref, out_ref, ggrad_ref, out_buf, ggrad_buf, sems):
+    copies = []
+    for h in range(mixed_ref.shape[1] // HD):
+        cols = slice(h * HD, (h + 1) * HD)
+        normed = mixed_ref[:, cols] * inv_ref[...]
+        sig = jax.nn.sigmoid(gate_ref[:, cols].astype(F32))
+        scale = gain_ref[:, cols] * sig
+        dn = dy_ref[:, cols].astype(F32) * scale
+        out_buf[:, cols] = (normed * scale).astype(BF16)
+        ggrad_buf[:, cols] = (dn * normed * (1.0 - sig)).astype(BF16)
         if h % 2 == 1:
             both = pl.ds((h - 1) * HD, PAIR)
             for j, (buf, ref) in enumerate(((out_buf, out_ref), (ggrad_buf, ggrad_ref))):
@@ -226,14 +232,24 @@
         compiler_params=params(16), name="forward",
     )(queries, keys, values, states, gain_row, gate, out_grad)
 
-    output, gate_grad, mixed_grad, own_after = pl.pallas_call(
+    mixed_grad, own_after, inv = pl.pallas_call(
         norm_kernel,
         in_specs=[VM] * 9,
-        out_specs=[HBM, HBM, VM, VM],
-        out_shape=[half_shape, half_shape, half_shape, state_shape],
-        scratch_shapes=[half_buf, half_buf, column, column, dma((2, pairs))],
-        compiler_params=params(16), name="norm",
+        out_specs=[VM, VM, VM],
+        out_shape=[half_shape, state_shape, jax.ShapeDtypeStruct((rows, HD), F32)],
+        scratch_shapes=[column],
+        compiler_params=params(12), name="norm",
     )(*tp_parts(sums), mixed, gate, gain_row, out_grad, queries)
+
+    output, gate_grad = pl.pallas_call(
+        output_kernel,
+        in_specs=[VM] * 5,
+        out_specs=[HBM, HBM],
+        out_shape=[half_shape, half_shape],
+        scratch_shapes=[half_buf, half_buf, dma((2, pairs))],
+        compiler_params=params(12), cost_estimate=cost(10**9, 8 * 2**20), name="output",
+    )(mixed, inv, gate, gain_row, out_grad)
+
     after = carried_in(own_after, True)
 
     q_grad, parts = pl.pallas_call(

time: 118 us -> 116 us (0.983)
  waiting for transfers between devices: 11.3 us -> 9.14 us
    all_to_all x1, waiting for transfers between devices: 6.71 us -> 4.59 us  [carried_in(): return lax.all_to_all(summed, 'ctx', 0, 0).reshape(value.shape)]
    pallas_call x1 -> x2, Pallas kernels: 2.77 us -> 3.43 us  [the longest x1 1.99 us: local(): pl.pallas_call(output_kernel, in_specs=[VM] * 5, out_specs=[HBM, HBM], ou...]
    unnamed x30 -> x40, local copies, waits for them, and re-layouts: 8.46 us -> 8.56 us
  transfers between devices with their start and end apart: 5 -> 5, of which waited for: 5 -> 5; matrix products, arithmetic and copies ran while one was open for 0% -> 0% of each run, Pallas kernels for 5% -> 6%
where the time goes in v4:
time: 116 us
  blocking collectives  71.6 us (62%)
  Pallas kernels  15.6 us (13%)
  starting transfers between devices  9.7 us (8%)
  waiting for transfers between devices  9.14 us (8%)
  local copies, waits for them, and re-layouts  8.56 us (7%)
    all_to_all x2, blocking collectives, carried_in(): mine = lax.all_to_all(value.reshape(count, rows, HD), 'ctx', 0, 0)  50 us
    all_to_all x1, blocking collectives, carried_in(): return lax.all_to_all(summed, 'ctx', 0, 0).reshape(value.shape)  21.6 us
    unnamed x40, local copies, waits for them, and re-layouts  8.56 us
    pallas_call x1, Pallas kernels, local(): pl.pallas_call(partial_kernel, in_specs=[VM] * 5, out_specs=[HBM, VM], ou...  5.38 us
    all_to_all x1, starting transfers between devices, carried_in(): return lax.all_to_all(summed, 'ctx', 0, 0).reshape(value.shape)  4.91 us
    ppermute x3, starting transfers between devices, tp_parts(): lax.ppermute(x, 'tp', [(i, i ^ flip) for i in range(n)])  4.7 us
    all_to_all x1, waiting for transfers between devices, carried_in(): return lax.all_to_all(summed, 'ctx', 0, 0).reshape(value.shape)  4.59 us
    ppermute x3, waiting for transfers between devices, tp_parts(): lax.ppermute(x, 'tp', [(i, i ^ flip) for i in range(n)])  3.4 us
  transfers between devices with their start and end apart: 5, of which 5 were waited for; matrix products, arithmetic and copies ran while one was open for 0% of the time, Pallas kernels for 6%

profile of v4, /device:TPU:32, one launch (start us, length us, event | category | flops | bytes accessed | tf_op | source)
XLA Modules:
  0.0 115.6 jit_solution(3444968799972972732)
XLA Ops:
  0.6 0.0 copy-start.2
  0.6 1.2 %copy-done.2 = bf16[512,1024]{1,0:T(8,128)(2,1)S(1)} copy-done((bf16[512,1024]{1,0:T(8,128)(2,1)S(1)}, bf16[512,1024]{1,0:T(8,128)(2,1)}, u32[]{:S(2)}) %copy-start.2) | copy-done | bytes 1048600
  1.9 1.2 %copy-done.4 = bf16[512,1024]{1,0:T(8,128)(2,1)S(1)} copy-done((bf16[512,1024]{1,0:T(8,128)(2,1)S(1)}, bf16[512,1024]{1,0:T(8,128)(2,1)}, u32[]{:S(2)}) %copy-start.4) | copy-done | bytes 1048600
  3.1 0.5 state.1
  3.6 0.0 copy-start.1
  3.6 0.0 copy-start.3
  3.7 29.0 %all_to_all.20.x = f32[32,32,128]{2,1,0:T(8,128)S(1)} all-to-all(f32[32,32,128]{2,1,0:T(8,128)S(1)} %bitcast.7), channel_id=1, replica_groups=mesh['ctx'=32,'tp'=8] {'ctx'}, dimensions={0} | all-to-all | bytes 1048576 | tf_op jit(solution)/shard_map/all_to_all | solution.py:188
  32.7 21.6 %all_to_all.21 = f32[32,32,128]{2,1,0:T(8,128)S(1)} all-to-all(f32[32,32,128]{2,1,0:T(8,128)S(1)} %prefix.1), channel_id=1, replica_groups=mesh['ctx'=32,'tp'=8] {'ctx'}, dimensions={0} | all-to-all | bytes 1048576 | tf_op jit(solution)/shard_map/all_to_all | solution.py:197
  54.4 3.1 %forward.1 = (f32[512,1024]{1,0:T(8,128)S(1)}, f32[2,512]{1,0:T(2,128)S(1)}) custom-call(bf16[512,1024]{1,0:T(8,128)(2,1)S(1)} %copy-done.10, bf16[512,1024]{1,0:T(8,128)(2,1)S(1)} %copy-done.3, bf16[512,1024]{1,0:T(8,128)(2,1)S(1)} %copy-done.5, f32[1024,128]{1,0:T(8,128)S(1)} %bitcast.5, f32[1,1024]{1,0:T(1,128)S(1)} %bitcast.9, ...), custom_call_target="tpu_custom_call" | custom-call | tf_op jit(solution)/shard_map/forward/pallas_call | solution.py:223
  57.5 0.1 collective-permute-start
  57.6 1.2 collective-permute-done
  58.7 2.8 %collective-permute-start.3 = (f32[2,512]{1,0:T(2,128)S(1)}, f32[2,512]{1,0:T(2,128)S(1)}, u32[]{:S(2)}, u32[]{:S(2)}) collective-permute-start(f32[2,512]{1,0:T(2,128)S(1)} %add.3.sums0_ref), channel_id=1, source_target_pairs={{0,6},{1,7},{2,4},{3,5},{4,2},{5,3},{6,0},{7,1},{8,14},{9,15},{10,... | collective-permute-start | bytes 12296 | tf_op jit(solution)/shard_map/ppermute | solution.py:203
  61.5 0.2 collective-permute-start.2
  61.7 1.7 %collective-permute-start.1 = (f32[2,512]{1,0:T(2,128)S(1)}, f32[2,512]{1,0:T(2,128)S(1)}, u32[]{:S(2)}, u32[]{:S(2)}) collective-permute-start(f32[2,512]{1,0:T(2,128)S(1)} %add.3.sums0_ref), channel_id=1, source_target_pairs={{0,4},{1,5},{2,6},{3,7},{4,0},{5,1},{6,2},{7,3},{8,12},{9,13},{10,... | collective-permute-start | bytes 12296 | tf_op jit(solution)/shard_map/ppermute | solution.py:203
  63.4 0.1 collective-permute-done.3.sums3_ref
  63.5 1.6 %collective-permute-done.2.sums2_ref = f32[2,512]{1,0:T(2,128)S(1)} collective-permute-done((f32[2,512]{1,0:T(2,128)S(1)}, f32[2,512]{1,0:T(2,128)S(1)}, u32[]{:S(2)}, u32[]{:S(2)}) %collective-permute-start.2) | collective-permute-done | bytes 4128 | tf_op jit(solution)/shard_map/ppermute | solution.py:203
  65.1 1.7 %collective-permute-done.1.sums1_ref = f32[2,512]{1,0:T(2,128)S(1)} collective-permute-done((f32[2,512]{1,0:T(2,128)S(1)}, f32[2,512]{1,0:T(2,128)S(1)}, u32[]{:S(2)}, u32[]{:S(2)}) %collective-permute-start.1) | collective-permute-done | bytes 4128 | tf_op jit(solution)/shard_map/ppermute | solution.py:203
  66.8 1.4 %norm.1 = (bf16[512,1024]{1,0:T(8,128)(2,1)S(1)}, f32[1024,128]{1,0:T(8,128)S(1)}, f32[512,128]{1,0:T(8,128)S(1)}) custom-call(f32[2,512]{1,0:T(2,128)S(1)} %add.3.sums0_ref, f32[2,512]{1,0:T(2,128)S(1)} %collective-permute-done.1.sums1_ref, f32[2,512]{1,0:T(2,128)S(1)} %collective-permute-done.2.sums2_ref, f32[2,512]{1,0:T(2,128)S(1)} %collective-permute-done.3.sums3_ref, ...), custom_call_target="tpu_custom_call" | custom-call | tf_op jit(solution)/shard_map/norm/pallas_call | solution.py:235
  68.3 0.0 copy-start.18
  68.3 21.0 %all_to_all.22.x = f32[32,32,128]{2,1,0:T(8,128)S(1)} all-to-all(f32[32,32,128]{2,1,0:T(8,128)S(1)} %bitcast.8), channel_id=1, replica_groups=mesh['ctx'=32,'tp'=8] {'ctx'}, dimensions={0} | all-to-all | bytes 1048576 | tf_op jit(solution)/shard_map/all_to_all | solution.py:188
  89.3 0.8 copy-done.16
  90.1 4.9 %all-to-all-start.3 = ((f32[32,32,128]{2,1,0:T(8,128)}), f32[32,32,128]{2,1,0:T(8,128)}, u32[]{:S(2)}, u32[]{:S(2)}) async-start(f32[32,32,128]{2,1,0:T(8,128)} %copy-done.16), calls=%async_computation.3 | async-start | bytes 1048576 | tf_op jit(solution)/shard_map/all_to_all | solution.py:197
  95.0 1.6 %copy-done.9 = f32[512,1024]{1,0:T(8,128)S(1)} copy-done((f32[512,1024]{1,0:T(8,128)S(1)}, f32[512,1024]{1,0:T(8,128)}, u32[]{:S(2)}) %copy-start.9) | copy-done | bytes 2097176
  96.6 2.0 %output.1 = (bf16[512,1024]{1,0:T(8,128)(2,1)}, bf16[512,1024]{1,0:T(8,128)(2,1)}) custom-call(f32[512,1024]{1,0:T(8,128)S(1)} %copy-done.9, f32[512,128]{1,0:T(8,128)S(1)} %get-tuple-element.18.inv_ref, bf16[512,1024]{1,0:T(8,128)(2,1)S(1)} %copy-done, f32[1,1024]{1,0:T(1,128)S(1)} %bitcast.11, bf16[512,1024]{1,0:T(8,128)(2,1)S(1)} %copy-done.1), custom_call_target="tpu_custom_call" | custom-call | flops 1000000000 | bytes 8388608 | tf_op jit(solution)/shard_map/output/pallas_call | solution.py:244
  98.6 0.3 copy-done.11
  98.9 0.1 copy-done.13
  99.0 0.3 copy-done.19
  99.4 5.4 %partial.1 = (bf16[512,1024]{1,0:T(8,128)(2,1)}, bf16[1024,1024]{1,0:T(8,128)(2,1)S(1)}) custom-call(bf16[512,1024]{1,0:T(8,128)(2,1)S(1)} %copy-done.11, bf16[512,1024]{1,0:T(8,128)(2,1)S(1)} %copy-done.3, bf16[512,1024]{1,0:T(8,128)(2,1)S(1)} %copy-done.6, f32[1024,128]{1,0:T(8,128)S(1)} %bitcast.6, bf16[512,1024]{1,0:T(8,128)(2,1)S(1)} %copy-done.19), custom_call_target="tpu_custom_call" | custom-call | flops 5000000000 | bytes 10485760 | tf_op jit(solution)/shard_map/partial/pallas_call | solution.py:255
  104.8 1.3 %copy-done.14 = bf16[1024,1024]{1,0:T(8,128)(2,1)} copy-done((bf16[1024,1024]{1,0:T(8,128)(2,1)}, bf16[1024,1024]{1,0:T(8,128)(2,1)S(1)}, u32[]{:S(2)}) %copy-start.14) | copy-done | bytes 2097176
  106.1 4.6 %all-to-all-done.3 = f32[32,32,128]{2,1,0:T(8,128)} async-done(((f32[32,32,128]{2,1,0:T(8,128)}), f32[32,32,128]{2,1,0:T(8,128)}, u32[]{:S(2)}, u32[]{:S(2)}) %all-to-all-start.3) | async-done | bytes 524320 | tf_op jit(solution)/shard_map/all_to_all | solution.py:197
  110.7 1.6 %copy-done.15 = bf16[1024,1024]{1,0:T(8,128)(2,1)S(1)} copy-done((bf16[1024,1024]{1,0:T(8,128)(2,1)S(1)}, bf16[1024,1024]{1,0:T(8,128)(2,1)}, u32[]{:S(2)}) %copy-start.15) | copy-done | bytes 2097176
  112.3 3.2 %gradient.1 = (bf16[512,1024]{1,0:T(8,128)(2,1)}, bf16[512,1024]{1,0:T(8,128)(2,1)}) custom-call(bf16[512,1024]{1,0:T(8,128)(2,1)S(1)} %copy-done.3, bf16[512,1024]{1,0:T(8,128)(2,1)S(1)} %copy-done.7, f32[1024,128]{1,0:T(8,128)} %bitcast.4.after_ref, bf16[1024,1024]{1,0:T(8,128)(2,1)S(1)} %copy-done.15), custom_call_target="tpu_custom_call" | custom-call | tf_op jit(solution)/shard_map/gradient/pallas_call | solution.py:263
  (30 shorter events, 0.1 us)
Async XLA Ops:
  0.6 1.2 %copy-start.2 = (bf16[512,1024]{1,0:T(8,128)(2,1)S(1)}, bf16[512,1024]{1,0:T(8,128)(2,1)}, u32[]{:S(2)}) copy-start(bf16[512,1024]{1,0:T(8,128)(2,1)} %k_ref.7) | copy-start | bytes 3145732
  1.9 1.2 %copy-start.4 = (bf16[512,1024]{1,0:T(8,128)(2,1)S(1)}, bf16[512,1024]{1,0:T(8,128)(2,1)}, u32[]{:S(2)}) copy-start(bf16[512,1024]{1,0:T(8,128)(2,1)} %v_ref.7) | copy-start | bytes 3145732
  3.1 51.2 %copy-start.5 = (bf16[512,1024]{1,0:T(8,128)(2,1)S(1)}, bf16[512,1024]{1,0:T(8,128)(2,1)}, u32[]{:S(2)}) copy-start(bf16[512,1024]{1,0:T(8,128)(2,1)} %v_ref.7) | copy-start | bytes 3145732
  3.1 51.2 %copy-start.10 = (bf16[512,1024]{1,0:T(8,128)(2,1)S(1)}, bf16[512,1024]{1,0:T(8,128)(2,1)}, u32[]{:S(2)}) copy-start(bf16[512,1024]{1,0:T(8,128)(2,1)} %q_ref.5) | copy-start | bytes 3145732
  3.6 50.7 %copy-start = (bf16[512,1024]{1,0:T(8,128)(2,1)S(1)}, bf16[512,1024]{1,0:T(8,128)(2,1)}, u32[]{:S(2)}) copy-start(bf16[512,1024]{1,0:T(8,128)(2,1)} %gate_ref.5) | copy-start | bytes 3145732
  3.6 50.7 %copy-start.1 = (bf16[512,1024]{1,0:T(8,128)(2,1)S(1)}, bf16[512,1024]{1,0:T(8,128)(2,1)}, u32[]{:S(2)}) copy-start(bf16[512,1024]{1,0:T(8,128)(2,1)} %dy_ref.5) | copy-start | bytes 3145732
  3.6 50.7 %copy-start.3 = (bf16[512,1024]{1,0:T(8,128)(2,1)S(1)}, bf16[512,1024]{1,0:T(8,128)(2,1)}, u32[]{:S(2)}) copy-start(bf16[512,1024]{1,0:T(8,128)(2,1)} %k_ref.7) | copy-start | bytes 3145732
  3.6 50.7 %copy-start.17 = (f32[1024]{0:T(1024)S(1)}, f32[1024]{0:T(1024)}, u32[]{:S(2)}) copy-start(f32[1024]{0:T(1024)} %param.10) | copy-start | bytes 12292
  54.3 3.1 %copy-start.12 = (f32[32,32,128]{2,1,0:T(8,128)}, f32[32,32,128]{2,1,0:T(8,128)S(1)}, u32[]{:S(2)}) copy-start(f32[32,32,128]{2,1,0:T(8,128)S(1)} %all_to_all.21) | copy-start | bytes 1572868
  57.5 10.8 %copy-start.8 = (f32[512,1024]{1,0:T(8,128)}, f32[512,1024]{1,0:T(8,128)S(1)}, u32[]{:S(2)}) copy-start(f32[512,1024]{1,0:T(8,128)S(1)} %get-tuple-element.16.mixed_ref) | copy-start | bytes 6291460
  57.5 1.3 %collective-permute-start = (f32[2,512]{1,0:T(2,128)S(1)}, f32[2,512]{1,0:T(2,128)S(1)}, u32[]{:S(2)}, u32[]{:S(2)}) collective-permute-start(f32[2,512]{1,0:T(2,128)S(1)} %get-tuple-element.17), channel_id=1, source_target_pairs={{0,1},{1,0},{2,3},{3,2},{4,5},{5,4},{6,7},{7,6},{8,9},{9,8},{10,11... | collective-permute-start | bytes 12296 | tf_op jit(solution)/shard_map/ppermute | solution.py:202
  58.7 4.8 %collective-permute-start.3 = (f32[2,512]{1,0:T(2,128)S(1)}, f32[2,512]{1,0:T(2,128)S(1)}, u32[]{:S(2)}, u32[]{:S(2)}) collective-permute-start(f32[2,512]{1,0:T(2,128)S(1)} %add.3.sums0_ref), channel_id=1, source_target_pairs={{0,6},{1,7},{2,4},{3,5},{4,2},{5,3},{6,0},{7,1},{8,14},{9,15},{10,... | collective-permute-start | bytes 12296 | tf_op jit(solution)/shard_map/ppermute | solution.py:203
  61.5 3.6 %collective-permute-start.2 = (f32[2,512]{1,0:T(2,128)S(1)}, f32[2,512]{1,0:T(2,128)S(1)}, u32[]{:S(2)}, u32[]{:S(2)}) collective-permute-start(f32[2,512]{1,0:T(2,128)S(1)} %add.3.sums0_ref), channel_id=1, source_target_pairs={{0,2},{1,3},{2,0},{3,1},{4,6},{5,7},{6,4},{7,5},{8,10},{9,11},{10,... | collective-permute-start | bytes 12296 | tf_op jit(solution)/shard_map/ppermute | solution.py:203
  61.7 5.1 %collective-permute-start.1 = (f32[2,512]{1,0:T(2,128)S(1)}, f32[2,512]{1,0:T(2,128)S(1)}, u32[]{:S(2)}, u32[]{:S(2)}) collective-permute-start(f32[2,512]{1,0:T(2,128)S(1)} %add.3.sums0_ref), channel_id=1, source_target_pairs={{0,4},{1,5},{2,6},{3,7},{4,0},{5,1},{6,2},{7,3},{8,12},{9,13},{10,... | collective-permute-start | bytes 12296 | tf_op jit(solution)/shard_map/ppermute | solution.py:203
  68.3 21.0 %copy-start.18 = (bf16[512,1024]{1,0:T(8,128)(2,1)}, bf16[512,1024]{1,0:T(8,128)(2,1)S(1)}, u32[]{:S(2)}) copy-start(bf16[512,1024]{1,0:T(8,128)(2,1)S(1)} %get-tuple-element.20.d_ref) | copy-start | bytes 3145732
  89.3 0.8 copy-start.16
  90.1 20.6 %all-to-all-start.3 = ((f32[32,32,128]{2,1,0:T(8,128)}), f32[32,32,128]{2,1,0:T(8,128)}, u32[]{:S(2)}, u32[]{:S(2)}) async-start(f32[32,32,128]{2,1,0:T(8,128)} %copy-done.16), calls=%async_computation.3 | async-start | bytes 1048576 | tf_op jit(solution)/shard_map/all_to_all | solution.py:197
  95.0 1.6 %copy-start.9 = (f32[512,1024]{1,0:T(8,128)S(1)}, f32[512,1024]{1,0:T(8,128)}, u32[]{:S(2)}) copy-start(f32[512,1024]{1,0:T(8,128)} %copy-done.8) | copy-start | bytes 6291460
  96.6 2.0 %copy-start.6 = (bf16[512,1024]{1,0:T(8,128)(2,1)S(1)}, bf16[512,1024]{1,0:T(8,128)(2,1)}, u32[]{:S(2)}) copy-start(bf16[512,1024]{1,0:T(8,128)(2,1)} %v_ref.7) | copy-start | bytes 3145732
  96.6 2.3 %copy-start.11 = (bf16[512,1024]{1,0:T(8,128)(2,1)S(1)}, bf16[512,1024]{1,0:T(8,128)(2,1)}, u32[]{:S(2)}) copy-start(bf16[512,1024]{1,0:T(8,128)(2,1)} %q_ref.5) | copy-start | bytes 3145732
  96.6 2.4 %copy-start.13 = (f32[32,32,128]{2,1,0:T(8,128)S(1)}, f32[32,32,128]{2,1,0:T(8,128)}, u32[]{:S(2)}) copy-start(f32[32,32,128]{2,1,0:T(8,128)} %copy-done.12) | copy-start | bytes 1572868
  96.6 2.8 %copy-start.19 = (bf16[512,1024]{1,0:T(8,128)(2,1)S(1)}, bf16[512,1024]{1,0:T(8,128)(2,1)}, u32[]{:S(2)}) copy-start(bf16[512,1024]{1,0:T(8,128)(2,1)} %copy-done.18) | copy-start | bytes 3145732
  99.4 11.3 %copy-start.7 = (bf16[512,1024]{1,0:T(8,128)(2,1)S(1)}, bf16[512,1024]{1,0:T(8,128)(2,1)}, u32[]{:S(2)}) copy-start(bf16[512,1024]{1,0:T(8,128)(2,1)} %v_ref.7) | copy-start | bytes 3145732
  104.8 1.4 %copy-start.14 = (bf16[1024,1024]{1,0:T(8,128)(2,1)}, bf16[1024,1024]{1,0:T(8,128)(2,1)S(1)}, u32[]{:S(2)}) copy-start(bf16[1024,1024]{1,0:T(8,128)(2,1)S(1)} %get-tuple-element.23.parts_ref) | copy-start | bytes 6291460
  110.7 1.6 %copy-start.15 = (bf16[1024,1024]{1,0:T(8,128)(2,1)S(1)}, bf16[1024,1024]{1,0:T(8,128)(2,1)}, u32[]{:S(2)}) copy-start(bf16[1024,1024]{1,0:T(8,128)(2,1)} %copy-done.14) | copy-start | bytes 6291460
